TPU v7x, 512 devices: a whole 4x4x16 slice. The times are simulated.
512 devices in a mesh: req: 32 (over y, z_lo), head: 16 (over x, z_hi, core).
Axes of the slice: x: 4, y: 4, z: 16 (z_hi: 2, z_lo: 8; z = z_hi * 8 + z_lo), core: 2. Of those that a mesh axis runs over, the one named last changes fastest.
Arguments:
- hidden: bfloat16 [256, 2048], P('req', 'head'), may hold values from -6 to 6
- attn_gain: float32 [2048], replicated, may hold values from 0.1 to 1.9
- q_weight: bfloat16 [2048, 2048], P(None, 'head'), may hold values from -0.125 to 0.125
- gate_weight: bfloat16 [2048, 2048], P(None, 'head'), may hold values from -0.125 to 0.125
- key_value_weight: bfloat16 [2048, 2048], P(None, 'head'), may hold values from -0.125 to 0.125
- q_gain: float32 [128], replicated, may hold values from 0.5 to 1.5
- k_gain: float32 [128], replicated, may hold values from 0.5 to 2
- out_weight: bfloat16 [2048, 2048], P('head'), may hold values from -0.5 to 0.5
- prompt_key_cache: bfloat16 [32, 4096, 8, 128], P('req', 'head'), may hold values from -3.5 to 3.5
- prompt_value_cache: bfloat16 [32, 4096, 8, 128], P('req', 'head'), may hold values from -6 to 6
- tail_key_cache: bfloat16 [32, 4, 256, 8, 128], P('req', None, 'head'), may hold values from -3.5 to 3.5
- tail_value_cache: bfloat16 [32, 4, 256, 8, 128], P('req', None, 'head'), may hold values from -6 to 6
- mlp_gain: float32 [2048], replicated, may hold values from 0.1 to 1.9
- mlp_gate: bfloat16 [2048, 6144], P('req', 'head'), may hold values from -0.125 to 0.125
- mlp_up: bfloat16 [2048, 6144], P('req', 'head'), may hold values from -0.125 to 0.125
- mlp_down: bfloat16 [6144, 2048], P('head'), may hold values from -0.109375 to 0.109375
- final_gain: float32 [2048], P('head'), may hold values from 0.1 to 1.9
- score_weight: float32 [2048], P('head'), may hold values from -0.125 to 0.125
- prompt_lengths: int32 [32], replicated, may hold values from 1 to 4096, 65536 in all
- tail_lengths: int32 [32, 4], replicated, may hold values from 1 to 256, 512 in all within a row
- group_prompt: int32 [32], replicated, may hold values from 0 to 31, each once
Outputs:
- new_hidden: bfloat16 [256, 2048], P('req', 'head')
- score: float32 [256], P('req')
Inputs may be any that keep to these rules, and one draw needn't show every extreme that they name: `group_prompt`: every prompt is held by exactly one group. `prompt_lengths`: one prompt has exactly 4096 prefix tokens. `tail_lengths`: in every prompt one continuation has exactly 256 tail tokens.
All inputs are finite; a program needn't handle non-finite values.
Results may differ from a plain program's by a relative error of at most 0.023.
Values may be sent and summed in bfloat16 or wider, within the bound.
A program may use at most 64 MiB of HBM per device.

v0:
```python
import math

import jax
import jax.numpy as jnp
from jax import lax
from jax.sharding import PartitionSpec as P

EPS = 1e-06
THETA = 1000000.0


def rms_scale(value, gain):
    return value * lax.rsqrt(jnp.mean(value * value, axis=-1, keepdims=True) + EPS) * gain


def rotate(value, position):
    head_width = value.shape[-1]
    half_width = head_width // 2
    frequency = jnp.exp(
        -math.log(THETA) * 2.0 * jnp.arange(half_width, dtype=jnp.float32) / head_width
    )
    angles = position.astype(jnp.float32)[:, None] * frequency[None, :]
    cosine = jnp.cos(angles)[:, None, :]
    sine_part = jnp.sin(angles)[:, None, :]
    first_half = value[..., :half_width]
    second_half = value[..., half_width:]
    return jnp.concatenate(
        [
            first_half * cosine - second_half * sine_part,
            second_half * cosine + first_half * sine_part,
        ],
        axis=-1,
    )


def shards(
    hidden,
    attn_gain,
    q_weight,
    gate_weight,
    key_value_weight,
    q_gain,
    k_gain,
    out_weight,
    prompt_key_cache,
    prompt_value_cache,
    tail_key_cache,
    tail_value_cache,
    mlp_gain,
    mlp_gate,
    mlp_up,
    mlp_down,
    final_gain,
    score_weight,
    prompt_lengths,
    tail_lengths,
    group_prompt,
):
    head_count = lax.axis_size("head")
    group_count = lax.axis_size("req")
    group_id = lax.axis_index("req")
    head_place = lax.axis_index("head")
    count_of_rows = hidden.shape[0]
    model_width = attn_gain.shape[0]
    head_width = q_gain.shape[0]
    own_heads = q_weight.shape[1] // head_width
    all_heads = own_heads * head_count
    block_count = key_value_weight.shape[1] // head_width
    kv_heads = block_count * head_count // 2
    sharing_count = all_heads // kv_heads
    cont_count = tail_lengths.shape[1]
    new_count = count_of_rows // cont_count
    score_scale = 1.0 / math.sqrt(head_width)
    slot_ids = jnp.arange(group_count, dtype=jnp.int32)
    prompt_id = jnp.sum(jnp.where(slot_ids == group_id, group_prompt, 0))
    prompt_len = jnp.sum(jnp.where(slot_ids == prompt_id, prompt_lengths, 0))
    tail_row = jnp.sum(jnp.where((slot_ids == prompt_id)[:, None], tail_lengths, 0), axis=0)
    owner_group = jnp.sum(
        jnp.where(group_prompt[None, :] == slot_ids[:, None], slot_ids[None, :], 0), axis=1
    )
    position = (
        prompt_len + tail_row[:, None] + jnp.arange(new_count, dtype=jnp.int32)[None, :]
    ).reshape(count_of_rows)
    whole_rows = lax.all_gather(hidden, "head", axis=1, tiled=True)
    block_rows = whole_rows.astype(jnp.float32)
    normalized_hidden = rms_scale(block_rows, attn_gain).astype(jnp.bfloat16)
    gate_pre = jnp.dot(normalized_hidden, gate_weight, preferred_element_type=jnp.float32)
    query_rows = jnp.dot(normalized_hidden, q_weight, preferred_element_type=jnp.float32).reshape(
        count_of_rows, own_heads, head_width
    )
    query_rows = rotate(rms_scale(query_rows, q_gain), position).astype(jnp.bfloat16)
    projected_rows = jnp.dot(
        normalized_hidden, key_value_weight, preferred_element_type=jnp.float32
    ).reshape(count_of_rows, block_count, head_width)
    is_key = (head_place * block_count + jnp.arange(block_count, dtype=jnp.int32)) % 2 == 0
    keyed = rotate(rms_scale(projected_rows, k_gain), position)
    fresh = jnp.where(is_key[None, :, None], keyed, projected_rows).astype(jnp.bfloat16)
    all_queries, all_fresh = (
        lax.all_gather(
            query_rows.reshape(count_of_rows, own_heads * head_width), "head", axis=1, tiled=True
        ),
        lax.all_gather(
            fresh.reshape(count_of_rows, block_count * head_width), "head", axis=1, tiled=True
        ),
    )
    query_groups = all_queries.reshape(count_of_rows, kv_heads, sharing_count, head_width)
    local_keys = prompt_key_cache[0]
    local_values = prompt_value_cache[0]
    span_length = local_keys.shape[0]
    block_size = min(128, span_length)
    block_total = span_length // block_size
    span_start = head_place * span_length

    def prefix_block(block_id, sums):
        numer_acc, total_acc = sums
        key_block = lax.dynamic_slice_in_dim(local_keys, block_id * block_size, block_size, 0)
        value_block = lax.dynamic_slice_in_dim(local_values, block_id * block_size, block_size, 0)
        scores = (
            jnp.einsum(
                "rkgd,tkd->rkgt", query_groups, key_block, preferred_element_type=jnp.float32
            )
            * score_scale
        )
        slot_pos = span_start + block_id * block_size + jnp.arange(block_size, dtype=jnp.int32)
        attention_weights = jnp.where(
            slot_pos[None, None, None, :] < prompt_len, jnp.exp(scores), 0.0
        )
        numer_acc = numer_acc + jnp.einsum(
            "rkgt,tkd->rkgd",
            attention_weights.astype(jnp.bfloat16),
            value_block,
            preferred_element_type=jnp.float32,
        )
        return (numer_acc, total_acc + jnp.sum(attention_weights, axis=-1))

    start_sums = (
        jnp.zeros((count_of_rows, kv_heads, sharing_count, head_width), jnp.float32),
        jnp.zeros((count_of_rows, kv_heads, sharing_count), jnp.float32),
    )
    numerator, denominator = lax.fori_loop(0, block_total, prefix_block, start_sums)
    continuation_rows = query_groups.reshape(
        cont_count, new_count, kv_heads, sharing_count, head_width
    )
    tkeys = tail_key_cache[0]
    tail_value_rows = tail_value_cache[0]
    tail_span = tkeys.shape[1]
    scores = (
        jnp.einsum(
            "cjkgd,ctkd->cjkgt", continuation_rows, tkeys, preferred_element_type=jnp.float32
        )
        * score_scale
    )
    tail_pos = head_place * tail_span + jnp.arange(tail_span, dtype=jnp.int32)
    tail_live = tail_pos[None, :] < tail_row[:, None]
    attention_weights = jnp.where(tail_live[:, None, None, None, :], jnp.exp(scores), 0.0)
    numerator = numerator + jnp.einsum(
        "ihbyw,iwbs->ihbys",
        attention_weights.astype(jnp.bfloat16),
        tail_value_rows,
        preferred_element_type=jnp.float32,
    ).reshape(count_of_rows, kv_heads, sharing_count, head_width)
    denominator = denominator + jnp.sum(attention_weights, axis=-1).reshape(
        count_of_rows, kv_heads, sharing_count
    )
    numerator = numerator.reshape(count_of_rows, all_heads, head_width)
    denominator = denominator.reshape(count_of_rows, all_heads)
    numer_sum, total_sum = lax.psum((numerator, denominator), "head")
    numer_own = lax.dynamic_slice_in_dim(numer_sum, head_place * own_heads, own_heads, 1)
    total_own = lax.dynamic_slice_in_dim(total_sum, head_place * own_heads, own_heads, 1)
    fresh_all = all_fresh.reshape(count_of_rows, kv_heads, 2, head_width)
    own_kv = max(own_heads // sharing_count, 1)
    per_kv = own_heads // own_kv
    nearby = lax.dynamic_slice_in_dim(fresh_all, head_place * own_heads // sharing_count, own_kv, 1)
    own_queries = query_rows.reshape(cont_count, new_count, own_kv, per_kv, head_width)
    recent_key_rows = nearby[:, :, 0].reshape(cont_count, new_count, own_kv, head_width)
    recent_value_rows = nearby[:, :, 1].reshape(cont_count, new_count, own_kv, head_width)
    scores = (
        jnp.einsum(
            "cjkgd,cukd->cjkgu", own_queries, recent_key_rows, preferred_element_type=jnp.float32
        )
        * score_scale
    )
    causal = (
        jnp.arange(new_count, dtype=jnp.int32)[None, :]
        <= jnp.arange(new_count, dtype=jnp.int32)[:, None]
    )
    attention_weights = jnp.where(causal[None, :, None, None, :], jnp.exp(scores), 0.0)
    numer_own = numer_own + jnp.einsum(
        "bfmne,beml->bfmnl",
        attention_weights.astype(jnp.bfloat16),
        recent_value_rows,
        preferred_element_type=jnp.float32,
    ).reshape(count_of_rows, own_heads, head_width)
    total_own = total_own + jnp.sum(attention_weights, axis=-1).reshape(count_of_rows, own_heads)
    attention = (numer_own / total_own[..., None]).reshape(count_of_rows, own_heads * head_width)
    gated = (attention * jax.nn.sigmoid(gate_pre)).astype(jnp.bfloat16)
    mixed = lax.psum(jnp.dot(gated, out_weight, preferred_element_type=jnp.float32), "head")
    attended = (block_rows + mixed).astype(jnp.bfloat16)
    col_width = model_width // head_count
    wide_rows = attended.astype(jnp.float32)
    mlp_in = rms_scale(wide_rows, mlp_gain).astype(jnp.bfloat16)
    column_in = lax.all_to_all(mlp_in, "req", split_axis=1, concat_axis=0, tiled=True)
    gate_part = jnp.dot(column_in, mlp_gate, preferred_element_type=jnp.float32)
    up_part = jnp.dot(column_in, mlp_up, preferred_element_type=jnp.float32)
    gate_own, up_own = (
        lax.psum_scatter(gate_part, "req", scatter_dimension=0, tiled=True),
        lax.psum_scatter(up_part, "req", scatter_dimension=0, tiled=True),
    )
    act_rows = (jax.nn.silu(gate_own) * up_own).astype(jnp.bfloat16)
    down_part = jnp.dot(act_rows, mlp_down, preferred_element_type=jnp.float32)
    down_total = lax.psum(down_part, "head")
    added = lax.dynamic_slice_in_dim(down_total, head_place * col_width, col_width, 1)
    residual = lax.dynamic_slice_in_dim(wide_rows, head_place * col_width, col_width, 1)
    finished = (residual + added).astype(jnp.bfloat16)
    everyone = lax.all_gather(finished, "req", axis=0, tiled=True)
    my_owner = jnp.sum(jnp.where(slot_ids == group_id, owner_group, 0))
    new_hidden = lax.dynamic_slice_in_dim(everyone, my_owner * count_of_rows, count_of_rows, 0)
    final_rows = new_hidden.astype(jnp.float32)
    squares, product = lax.psum(
        (
            jnp.sum(final_rows * final_rows, axis=-1),
            jnp.sum(final_rows * final_gain * score_weight, axis=-1),
        ),
        "head",
    )
    score = product * lax.rsqrt(squares / model_width + EPS)
    return (new_hidden, score)


def solution(mesh):
    return jax.shard_map(
        shards,
        mesh=mesh,
        in_specs=(
            P("req", "head"),
            P(),
            P(None, "head"),
            P(None, "head"),
            P(None, "head"),
            P(),
            P(),
            P("head", None),
            P("req", "head", None, None),
            P("req", "head", None, None),
            P("req", None, "head", None, None),
            P("req", None, "head", None, None),
            P(),
            P("req", "head"),
            P("req", "head"),
            P("head", None),
            P("head"),
            P("head"),
            P(),
            P(),
            P(),
        ),
        out_specs=(P("req", "head"), P("req")),
        check_vma=False,
    )
```

profile of v0, /device:TPU:1, one launch (start us, length us, event | category | flops | bytes accessed | tf_op | source)
XLA Modules:
  0.0 1502.3 jit_solution(17086110039047880849)
XLA Ops:
  7.3 51.2 %all_gather.12 = bf16[8,2048]{1,0:T(8,128)(2,1)S(1)} all-gather(bf16[8,128]{1,0:T(8,128)(2,1)} %param.23), channel_id=1, replica_groups=mesh['req'=32,'head'=16] {'head'}, dimensions={1}, use_global_device_ids=true | all-gather | bytes 34816 | tf_op jit(solution)/shard_map/all_gather | solution.py:84
  58.4 0.1 fusion.23
  58.6 0.8 select_reduce_fusion
  59.3 1.3 fusion.70
  60.6 0.6 iota_compare_fusion.2
  61.3 2.0 select_reduce_fusion.2
  63.3 0.8 select_reduce_fusion.1
  64.1 0.7 broadcast_add_fusion
  64.8 0.1 add_convert_fusion.1
  64.9 0.1 convert_element_type.64
  65.0 1.4 multiply_reduce_fusion.2
  66.4 0.7 multiply_bitcast_fusion.1
  67.1 0.1 fusion.50
  67.2 0.1 pad_maximum_fusion
  67.3 33.8 %all_gather.13 = bf16[8,2048]{1,0:T(8,128)(2,1)S(1)} all-gather(bf16[8,128]{1,0:T(8,128)(2,1)S(1)} %pad_maximum_fusion), channel_id=1, replica_groups=mesh['req'=32,'head'=16] {'head'}, dimensions={1}, use_global_device_ids=true | all-gather | bytes 34816 | tf_op jit(solution)/shard_map/all_gather | solution.py:99
  101.1 1.4 copy_bitcast_fusion
  102.6 2.6 while.16
  102.6 0.8 add_compare_fusion.2
  103.3 0.3 fusion.110
  103.7 0.2 fusion.111
  103.9 0.7 add_compare_fusion.2
  104.6 0.3 fusion.110
  105.0 0.2 fusion.111
  105.2 0.1 broadcast_compare_fusion
  105.3 0.3 fusion.85
  105.6 1.1 convolution_bitcast_fusion.1
  106.8 0.6 copy.83
  107.6 0.3 multiply_reduce_fusion.1
  107.9 0.1 multiply_bitcast_fusion
  108.0 0.1 fusion.54
  108.1 0.1 fusion.57
  108.2 43.8 %all_gather.14 = bf16[8,2048]{1,0:T(8,128)(2,1)S(1)} all-gather(bf16[8,128]{1,0:T(8,128)(2,1)S(1)} %fusion.57), channel_id=1, replica_groups=mesh['req'=32,'head'=16] {'head'}, dimensions={1}, use_global_device_ids=true | all-gather | bytes 34816 | tf_op jit(solution)/shard_map/all_gather | solution.py:102
  152.1 0.2 fusion.14
  152.3 0.1 copy.84
  152.4 0.1 fusion.66
  152.4 0.1 fusion.68
  152.5 0.1 copy.90
  152.6 0.1 reshape.317
  152.7 0.1 copy.88
  152.8 0.1 copy.87
  152.9 0.1 copy.89
  153.0 62.0 %psum.43 = f32[8,16]{0,1:T(8,128)S(1)} all-reduce(f32[8,16]{0,1:T(8,128)S(1)} %bitcast.127), channel_id=1, replica_groups=mesh['req'=32,'head'=16] {'head'}, use_global_device_ids=true, to_apply=%region_11.12 | all-reduce | flops 128 | bytes 1024 | tf_op jit(solution)/shard_map/psum | solution.py:167
  215.0 0.1 copy.86
  215.1 0.1 fusion.88
  215.2 132.7 %all-reduce.9.cloned.1.call-done = f32[8,16,128]{2,0,1:T(8,128)} async-done(((f32[8,16,128]{2,0,1:T(8,128)}), f32[8,16,128]{2,0,1:T(8,128)}) %all-reduce.9.cloned.1.call-update) | async-done | bytes 65552 | tf_op jit(solution)/shard_map/psum | solution.py:167
  347.9 1.7 fusion.20
  349.7 242.6 %all-reduce.11.cloned.1.call-done = f32[8,2048]{1,0:T(8,128)} async-done(((f32[8,2048]{1,0:T(8,128)}), f32[8,2048]{1,0:T(8,128)}) %all-reduce.11.cloned.1.call-update) | async-done | bytes 65552 | tf_op jit(solution)/shard_map/psum | solution.py:197
  592.3 1.0 multiply_reduce_fusion
  593.3 0.1 multiply_convert_fusion
  593.4 0.1 all_to_all.14
  593.6 0.1 reshape.325
  593.7 16.2 %all_to_all.19 = bf16[32,2,256]{2,1,0:T(2,128)(2,1)S(1)} all-to-all(bf16[32,2,256]{2,1,0:T(2,128)(2,1)S(1)} %reshape.325), channel_id=1, replica_groups=mesh['req'=32,'head'=16] {'req'}, dimensions={0} | all-to-all | bytes 65536 | tf_op jit(solution)/shard_map/all_to_all | solution.py:202
  609.9 0.1 reshape.326
  610.1 0.9 fusion.27
  611.0 1.0 fusion.29
  612.0 1.3 dynamic-slice
  613.9 428.9 %all-reduce.15.cloned.1.call-done = (f32[256,384]{1,0:T(8,128)}, f32[256,384]{1,0:T(8,128)}) async-done(((f32[256,384]{1,0:T(8,128)}, f32[256,384]{1,0:T(8,128)}), (f32[256,384]{1,0:T(8,128)}, f32[256,384]{1,0:T(8,128)})) %all-reduce.15.cloned.1.call-update) | async-done | bytes 786448
  1042.8 1.7 fusion.35
  1045.2 263.3 %all-reduce.13.cloned.1.call-done = f32[8,2048]{1,0:T(8,128)} async-done(((f32[8,2048]{1,0:T(8,128)}), f32[8,2048]{1,0:T(8,128)}) %all-reduce.13.cloned.1.call-update) | async-done | bytes 65552 | tf_op jit(solution)/shard_map/psum | solution.py:211
  1308.5 0.7 add_convert_fusion
  1309.2 101.1 %all_gather.15 = bf16[256,128]{1,0:T(8,128)(2,1)S(1)} all-gather(bf16[8,128]{1,0:T(8,128)(2,1)S(1)} %add_convert_fusion), channel_id=1, replica_groups=mesh['req'=32,'head'=16] {'req'}, dimensions={0}, use_global_device_ids=true | all-gather | bytes 67584 | tf_op jit(solution)/shard_map/all_gather | solution.py:215
  1410.2 0.7 fusion.48
  1411.0 84.3 %all-reduce.3 = (f32[8]{0:T(128)S(1)}, f32[8]{0:T(128)S(1)}) all-reduce(f32[8]{0:T(128)S(1)} %get-tuple-element.172, f32[8]{0:T(128)S(1)} %get-tuple-element.171), channel_id=1, replica_groups=mesh['req'=32,'head'=16] {'head'}, use_global_device_ids=true, to_apply=%region_21.22 | all-reduce | flops 16 | bytes 128 | tf_op jit(solution)/shard_map/psum | solution.py:219
  1495.3 0.5 rsqrt_multiply_fusion
  (50 shorter events, 0.5 us)
Async XLA Ops:
  7.2 1035.7 %copy-start = (bf16[384,2048]{1,0:T(8,128)(2,1)S(1)}, bf16[384,2048]{1,0:T(8,128)(2,1)}, u32[]{:S(2)}) copy-start(bf16[384,2048]{1,0:T(8,128)(2,1)} %param.38) | copy-start | bytes 4718596
  7.2 340.7 %all-reduce.9.cloned.1.call-start = ((), (), s32[]{:S(2)}) async-start(), calls=%async_computation.1 | async-start | bytes 131072 | tf_op jit(solution)/shard_map/psum | solution.py:167
  102.5 2.8 copy-start.11
  102.5 5.0 copy-start.3
  102.5 5.0 copy-start.4
  105.2 2.8 copy-start.8
  105.2 242.7 %copy-start.1 = (bf16[128,2048]{1,0:T(8,128)(2,1)S(1)}, bf16[128,2048]{1,0:T(8,128)(2,1)}, u32[]{:S(2)}) copy-start(bf16[128,2048]{1,0:T(8,128)(2,1)} %param.30) | copy-start | bytes 1572868
  105.2 242.7 %copy-start.2 = (bf16[2048,128]{1,0:T(8,128)(2,1)S(1)}, bf16[2048,128]{1,0:T(8,128)(2,1)}, u32[]{:S(2)}) copy-start(bf16[2048,128]{1,0:T(8,128)(2,1)} %param.26) | copy-start | bytes 1572868
  105.6 487.7 %copy-start.7 = (f32[2048]{0:T(1024)S(1)}, f32[2048]{0:T(1024)}, u32[]{:S(2)}) copy-start(f32[2048]{0:T(1024)} %param.35) | copy-start | bytes 24580
  106.8 503.3 %copy-start.5 = (bf16[64,384]{1,0:T(8,128)(2,1)S(1)}, bf16[64,384]{1,0:T(8,128)(2,1)}, u32[]{:S(2)}) copy-start(bf16[64,384]{1,0:T(8,128)(2,1)} %param.37) | copy-start | bytes 147460
  107.4 484.9 %all-reduce.11.cloned.1.call-start = ((), (), s32[]{:S(2)}) async-start(), calls=%async_computation.2 | async-start | bytes 131072 | tf_op jit(solution)/shard_map/psum | solution.py:197
  107.6 503.4 %copy-start.6 = (bf16[64,384]{1,0:T(8,128)(2,1)S(1)}, bf16[64,384]{1,0:T(8,128)(2,1)}, u32[]{:S(2)}) copy-start(bf16[64,384]{1,0:T(8,128)(2,1)} %param.36) | copy-start | bytes 147460
  349.7 693.2 %all-reduce.15.cloned.1.call-start = ((), (), s32[]{:S(2)}) async-start(), calls=%async_computation.4 | async-start | bytes 1572864
  611.0 799.3 %copy-start.9 = (f32[128]{0:T(128)S(1)}, f32[128]{0:T(128)}, u32[]{:S(2)}) copy-start(f32[128]{0:T(128)} %param.40) | copy-start | bytes 1540
  611.0 799.3 %copy-start.10 = (f32[128]{0:T(128)S(1)}, f32[128]{0:T(128)}, u32[]{:S(2)}) copy-start(f32[128]{0:T(128)} %param.39) | copy-start | bytes 1540
  612.0 696.5 %all-reduce.13.cloned.1.call-start = ((), (), s32[]{:S(2)}) async-start(), calls=%async_computation.3 | async-start | bytes 131072 | tf_op jit(solution)/shard_map/psum | solution.py:211
Sparse Core Ops, SparseCore 0:
  107.6 240.3 all-reduce.8
  351.1 241.2 all-reduce.10
  612.1 430.6 all-reduce.14
  1045.9 262.5 all-reduce.12
where the time goes:
time: 1500 us
  waiting for transfers between devices  1070 us (71%)
  blocking collectives  392 us (26%)
  between operations  15.4 us (1%)
    unnamed x5, waiting for transfers between devices  429 us
    psum x1, waiting for transfers between devices, shards(): down_total = lax.psum(down_part, 'head')  263 us
    psum x1, waiting for transfers between devices, shards(): lax.psum(jnp.dot(gated, out_weight, preferred_element_type=jnp.float32),...  243 us
    psum x1, waiting for transfers between devices, shards(): numer_sum, total_sum = lax.psum((numerator, denominator), 'head')  133 us
    all_gather x1, blocking collectives, shards(): everyone = lax.all_gather(finished, 'req', axis=0, tiled=True)  101 us
    psum x1, blocking collectives, shards(): lax.psum((jnp.sum(final_rows * final_rows, axis=-1), jnp.sum(final_rows *...  84.3 us
    psum x1, blocking collectives, shards(): numer_sum, total_sum = lax.psum((numerator, denominator), 'head')  62 us
    all_gather x1, blocking collectives, shards(): whole_rows = lax.all_gather(hidden, 'head', axis=1, tiled=True)  51.2 us
  transfers between devices with their start and end apart: 4, of which 4 were waited for; matrix products, arithmetic and copies ran while one was open for 0% of the time, Pallas kernels for 0%

commit v1 on v0

v1 whole, which is shorter than its diff:
```python
import functools
import math

import jax
import jax.numpy as jnp
from jax import lax
from jax.experimental import pallas as pl
from jax.experimental.pallas import tpu as pltpu
from jax.sharding import PartitionSpec as P

EPS = 1e-06
THETA = 1000000.0
MESH = pl.DeviceIdType.MESH
BF = jnp.bfloat16
F32 = jnp.float32
WIDTH = 2048
SCALE = 1.0 / math.sqrt(128.0)

NEAR = [(2, 1), (2, 0), (1, 1), (3, 1), (1, 0), (3, 0), (0, 1)]
FAR = [(2, 1), (2, 0), (1, 1), (3, 1), (1, 0), (3, 0), (0, 1), (0, 0)]


def dot(a, b):
    return jnp.dot(a, b, preferred_element_type=F32)


def dot_nt(a, b):
    return lax.dot_general(a, b, (((1,), (1,)), ((), ())), preferred_element_type=F32)


def kernel(
    plen_ref, tlen_ref, gp_ref,
    hidden_ref, again_ref, qgain_ref, kgain_ref, mgain_ref, fgain_ref, sw_ref,
    wq_hbm, wg_hbm, wkv_hbm, wo_hbm, pk_hbm, pv_hbm, tk_hbm, tv_hbm, mg_hbm, mu_hbm, md_hbm,
    out_ref, score_ref,
    wq, wg, wkv, wo, kc, vc, wgate, wup, wdown,
    hb, hf, qs, qb, qf, fs, fb, mb, mf, nb, nf, sb, rb, tb, xb, ps, pb, ds_, db, ys, yb, zs, zb_, cs, cb, gs, gb,
    lsem, ssem, rsem,
):
    r = lax.axis_index("req")
    h = lax.axis_index("head")
    y, z = r // 8, r % 8
    x, zh, c = h // 4, (h // 2) % 2, h % 2
    zz, zb = z // 2, z % 2
    n = x * 2 + c
    oh = 1 - zh

    def head_at(dx, dz, dc):
        return ((x + dx) % 4) * 4 + ((zh + dz) % 2) * 2 + (c + dc) % 2

    def near_at(dx, dc):
        return ((x + dx) % 4) * 2 + (c + dc) % 2

    def send(src, dst, phase, at, dev):
        pltpu.make_async_remote_copy(
            src_ref=src, dst_ref=dst, send_sem=ssem.at[phase], recv_sem=rsem.at[at],
            device_id=dev, device_id_type=MESH,
        ).start()

    def waiter(ref, phase, at):
        return pltpu.make_async_remote_copy(
            src_ref=ref, dst_ref=ref, send_sem=ssem.at[phase], recv_sem=rsem.at[at],
            device_id=(r, head_at(0, 0, 1)), device_id_type=MESH,
        )

    def wait_recv(ref, at):
        waiter(ref, 0, at).wait_recv()

    def wait_send(ref, phase):
        waiter(ref, phase, 0).wait_send()

    own_w = y * 2 + zb
    local = [
        (mg_hbm, wgate.at[own_w]), (mu_hbm, wup.at[own_w]),
        (wq_hbm, wq), (wg_hbm, wg), (wkv_hbm, wkv),
        (pk_hbm, kc.at[pl.ds(0, 2048)]), (tk_hbm, kc.at[pl.ds(2048, 512)]),
        (pv_hbm, vc.at[pl.ds(0, 2048)]), (tv_hbm, vc.at[pl.ds(2048, 512)]),
        (wo_hbm, wo), (md_hbm, wdown),
    ]
    copies = [pltpu.make_async_copy(s, d, lsem.at[i]) for i, (s, d) in enumerate(local)]
    for cp in copies:
        cp.start()

    bar = pltpu.get_barrier_semaphore()

    def greet(dev):
        pl.semaphore_signal(bar, inc=1, device_id=dev, device_id_type=MESH)

    for dzl in range(1, 8):
        for dz in (1, 0):
            greet((y * 8 + (z + dzl) % 8, head_at(0, dz, 0)))
    for dzz in (2, 1, 3, 0):
        for dz in (1, 0):
            for dc in (1, 0):
                dev = (y * 8 + ((zz + dzz) % 4) * 2 + zb, zz * 4 + ((zh + dz) % 2) * 2 + (c + dc) % 2)
                if dzz == 0 and dz == 0 and dc == 0:
                    @pl.when(x != zz)
                    def _():
                        greet(dev)
                else:
                    greet(dev)
    for dx, dc in FAR:
        greet((r, head_at(dx, 1, dc)))
    for dx, dc in NEAR:
        greet((r, head_at(dx, 0, dc)))
    for dy in (2, 1, 3):
        for dzb in (1, 0):
            greet((((y + dy) % 4) * 8 + zz * 2 + (zb + dzb) % 2, h))

    hb[n] = hidden_ref[...]
    gs[...] = jnp.broadcast_to(fgain_ref[...] * sw_ref[...], (8, 128))

    prompt = gp_ref[r]
    plen = plen_ref[prompt]
    tails = [tlen_ref[prompt, i] for i in range(4)]

    def find(g, found):
        value = gp_ref[g]
        mine = jnp.where(value == r, g, found[8])
        return tuple(jnp.where(value == y * 8 + i, g, found[i]) for i in range(8)) + (mine,)

    owners = lax.fori_loop(0, 32, find, (jnp.int32(0),) * 9)

    row = lax.broadcasted_iota(jnp.int32, (8, 128), 0)
    lane = lax.broadcasted_iota(jnp.int32, (8, 128), 1)
    position = plen + row % 2
    for i in range(4):
        position = position + jnp.where(row // 2 == i, tails[i], 0)
    half_lane = (lane % 64).astype(F32)
    frequency = jnp.exp(-math.log(THETA) * 2.0 * half_lane / 128.0)
    angle = position.astype(F32) * frequency
    cosine = jnp.cos(angle)
    sine = jnp.sin(angle)
    sine = jnp.where(lane < 64, -sine, sine)

    def normed_rotated(value, gain):
        value = value * lax.rsqrt(jnp.mean(value * value, axis=-1, keepdims=True) + EPS) * gain
        return value * cosine + pltpu.roll(value, 64, 1) * sine

    pl.semaphore_wait(bar, 50 + jnp.where(x != zz, 1, 0))

    for dx, dc in FAR:
        send(hidden_ref, hf.at[n], 15, 1, (r, head_at(dx, 1, dc)))
    for dx, dc in NEAR:
        send(hidden_ref, hb.at[n], 0, 0, (r, head_at(dx, 0, dc)))
    send(gs, gb.at[zh], 11, 20, (r, head_at(0, 1, 0)))
    gb[zh] = gs[...]

    copies[0].wait()
    copies[1].wait()
    for dy in (2, 1, 3, 0):
        for dzb in (1, 0):
            if dy or dzb:
                dev = (((y + dy) % 4) * 8 + zz * 2 + (zb + dzb) % 2, h)
                send(wgate.at[own_w], wgate.at[own_w], 12, 21, dev)
                send(wup.at[own_w], wup.at[own_w], 13, 22, dev)

    for i in range(2, 11):
        copies[i].wait()

    def features(half, at):
        place = at * 4 + half * 2
        offset = pl.multiple_of(place * 128, 256)
        ref = hb if half is zh else hf
        value = jnp.concatenate([ref[at * 2].astype(F32), ref[at * 2 + 1].astype(F32)], axis=1)
        scaled = (value * again_ref[:, pl.ds(offset, 256)]).astype(BF)
        return value * value, scaled, offset

    wait_recv(hb.at[pl.ds(0, 7)], 0)
    squares = jnp.zeros((8, 256), F32)
    q_acc = jnp.zeros((8, 128), F32)
    g_acc = jnp.zeros((8, 128), F32)
    kv_acc = jnp.zeros((8, 128), F32)
    for i in range(4):
        square, scaled, offset = features(zh, i)
        squares = squares + square
        q_acc = q_acc + dot(scaled, wq[pl.ds(offset, 256), :])
        g_acc = g_acc + dot(scaled, wg[pl.ds(offset, 256), :])
        kv_acc = kv_acc + dot(scaled, wkv[pl.ds(offset, 256), :])
    wait_recv(hf, 1)
    rest = []
    for i in range(4):
        square, scaled, offset = features(oh, i)
        squares = squares + square
        rest.append((scaled, offset))
        q_acc = q_acc + dot(scaled, wq[pl.ds(offset, 256), :])
    row_scale = lax.rsqrt(jnp.sum(squares, axis=-1, keepdims=True) / WIDTH + EPS)
    query = normed_rotated(q_acc * row_scale, qgain_ref[...]).astype(BF)
    qs[...] = query
    qb[n] = query

    for dx, dc in FAR:
        send(qs, qf.at[n], 16, 3, (r, head_at(dx, 1, dc)))
    for dx, dc in NEAR:
        send(qs, qb.at[n], 1, 2, (r, head_at(dx, 0, dc)))

    for scaled, offset in rest:
        g_acc = g_acc + dot(scaled, wg[pl.ds(offset, 256), :])
        kv_acc = kv_acc + dot(scaled, wkv[pl.ds(offset, 256), :])
    gate = jax.nn.sigmoid(g_acc * row_scale)
    projected = kv_acc * row_scale
    fresh = jnp.where(c == 0, normed_rotated(projected, kgain_ref[...]), projected).astype(BF)
    fs[...] = fresh
    fb[c] = fresh
    send(fs, fb.at[c], 2, 4, (r, head_at(0, 0, 1)))

    def attend(half, queries, sums):
        q = queries[...].astype(F32).reshape(64, 128).astype(BF)

        def weights(keys, live):
            scores = dot_nt(q, keys) * SCALE
            rows = lax.broadcasted_iota(jnp.int32, scores.shape, 0)
            cols = lax.broadcasted_iota(jnp.int32, scores.shape, 1)
            seen = ((cols & 7) == (rows >> 4) * 2 + half) & live(rows, cols)
            return jnp.where(seen, jnp.exp(scores), 0.0)

        def tail_live(rows, cols):
            limit = jnp.where(cols < 256, jnp.where(cols < 128, tails[0], tails[1]),
                              jnp.where(cols < 384, tails[2], tails[3])) - h * 16
            return ((cols >> 7) == ((rows & 7) >> 1)) & (((cols >> 3) & 15) < limit)

        w_prefix = weights(kc[pl.ds(0, 2048), :], lambda rows, cols: (cols >> 3) < plen - h * 256)
        w_tail = weights(kc[pl.ds(2048, 512), :], tail_live)
        numer = dot(w_prefix.astype(BF), vc[pl.ds(0, 2048), :]) + dot(w_tail.astype(BF), vc[pl.ds(2048, 512), :])
        total = jnp.sum(w_prefix, axis=-1, keepdims=True) + jnp.sum(w_tail, axis=-1, keepdims=True)
        high = total.astype(BF).astype(F32)
        lanes = lax.broadcasted_iota(jnp.int32, (64, 128), 1)
        totals = jnp.where(lanes < 64, high, total - high)
        both = jnp.concatenate([numer.reshape(8, 8, 128), totals.reshape(8, 8, 128)], axis=1)
        sums[...] = both.astype(BF)

    wait_recv(qb.at[pl.ds(0, 7)], 2)
    attend(zh, qb, mb)
    nb[n] = mb[n]
    for dx, dc in NEAR:
        send(mb.at[near_at(dx, dc)], nb.at[n], 3, 5, (r, head_at(dx, 0, dc)))
    wait_recv(qf, 3)
    attend(oh, qf, mf)
    for dx, dc in FAR:
        send(mf.at[near_at(dx, dc)], nf.at[n], 17, 6, (r, head_at(dx, 1, dc)))

    wait_recv(fb.at[0], 4)
    scores = dot_nt(query, fb[0]) * SCALE
    rows = lax.broadcasted_iota(jnp.int32, (8, 8), 0)
    cols = lax.broadcasted_iota(jnp.int32, (8, 8), 1)
    w_fresh = jnp.where((rows // 2 == cols // 2) & (cols <= rows), jnp.exp(scores), 0.0)
    numer = dot(w_fresh.astype(BF), fb[1])
    total = jnp.sum(w_fresh, axis=-1, keepdims=True)

    wait_recv(nb.at[pl.ds(0, 7)], 5)
    sums = jnp.sum(nb[...].astype(F32), axis=0)
    wait_recv(nf, 6)
    sums = sums + jnp.sum(nf[...].astype(F32), axis=0)
    numer = numer + sums[:8]
    total = total + sums[8:, 0:1] + sums[8:, 64:65]
    gated = (numer / total * gate).astype(BF)

    mixed = dot(gated, wo[...])
    for place in range(8):
        px, pc = place // 2, place % 2
        for j, block in enumerate((8 * pc + px, 8 * pc + 4 + px, 4 * px + pc, 4 * px + 2 + pc)):
            sb[place, j] = mixed[:, block * 128:(block + 1) * 128].astype(BF)
    rb[n] = sb[n]
    for dx, dc in NEAR:
        send(sb.at[near_at(dx, dc)], rb.at[n], 4, 7, (r, head_at(dx, 0, dc)))
    wait_recv(rb.at[pl.ds(0, 7)], 7)
    sums = jnp.sum(rb[...].astype(F32), axis=0)
    first = jnp.where(zh == 0, 1.0, 0.0)

    def hidden_at(place):
        both = jnp.where(x // 2 == 0, hb[place].astype(F32), hf[place].astype(F32))
        return both * first

    tb[0] = (sums[0] + hidden_at(4 * c + x % 2)).astype(BF)
    tb[1] = (sums[1] + hidden_at(4 * c + 2 + x % 2)).astype(BF)
    residual = [sums[2] + hb[n].astype(F32) * first, sums[3] + hf[n].astype(F32) * first]

    slot = (zh * 4 + zz) * 2 + c
    target = y * 8 + 2 * x + zb
    for dz in (1, 0):
        for dx, dc in FAR:
            if dz or dx or dc:
                send(tb, xb.at[slot], 5, 8, (target, head_at(dx, dz, dc)))

    @pl.when(x != zz)
    def _():
        send(tb, xb.at[slot], 14, 8, (target, h))

        wait_recv(xb, 8)

    @pl.when(x == zz)
    def _():
        xb[slot] = tb[...]
        wait_recv(xb.at[pl.ds(0, 15)], 8)

    halves = xb[...].astype(F32)
    attended = halves[:8] + halves[8:]
    squares = jnp.zeros((32, 128), F32)
    parts = []
    for fy in range(4):
        block = jnp.concatenate([attended[i * 2 + fy // 2, fy % 2] for i in range(4)], axis=0)
        squares = squares + block * block
        offset = pl.multiple_of((fy * 4 + zz) * 128, 128)
        parts.append((block * mgain_ref[:, pl.ds(offset, 128)]).astype(BF))
    mlp_in = jnp.concatenate(parts, axis=1)
    square = jnp.sum(squares, axis=-1, keepdims=True)
    high = square.astype(BF).astype(F32)
    lanes = lax.broadcasted_iota(jnp.int32, (32, 128), 1)
    square = jnp.where(lanes < 64, high, square - high)
    wait_recv(wgate.at[pl.ds(0, 7)], 21)
    wait_recv(wup.at[pl.ds(0, 7)], 22)
    gate_part = dot(mlp_in, wgate[...].reshape(512, 384))
    up_part = dot(mlp_in, wup[...].reshape(512, 384))

    for i in range(4):
        rows = slice(i * 8, i * 8 + 8)
        ps[i, :, 0:384] = gate_part[rows].astype(BF)
        ps[i, :, 384:768] = up_part[rows].astype(BF)
        ps[i, :, 768:896] = square[rows].astype(BF)
    pb[zz] = ps[zz]
    for dzz in (2, 1, 3):
        to = (zz + dzz) % 4
        send(ps.at[to], pb.at[zz], 6, 9, (y * 8 + 2 * to + zb, h))
    wait_recv(pb.at[pl.ds(0, 3)], 9)
    sums = jnp.sum(pb[...].astype(F32), axis=0)
    scale = lax.rsqrt((sums[:, 768:769] + sums[:, 832:833]) / WIDTH + EPS)
    act = (jax.nn.silu(sums[:, 0:384] * scale) * (sums[:, 384:768] * scale)).astype(BF)

    down = dot(act, wdown[...])
    for place in range(8):
        px, pc = place // 2, place % 2
        for j, block in enumerate((4 * px + pc, 4 * px + 2 + pc)):
            ds_[place, j] = down[:, block * 128:(block + 1) * 128].astype(BF)
    db[n] = ds_[n]
    for dx, dc in NEAR:
        send(ds_.at[near_at(dx, dc)], db.at[n], 7, 10, (r, head_at(dx, 0, dc)))
    wait_recv(db.at[pl.ds(0, 7)], 10)
    sums = jnp.sum(db[...].astype(F32), axis=0)
    for j in range(2):
        value = (sums[j] + residual[j]).astype(BF)
        ys[j] = value
        yb[y, j] = value

    for dy in (2, 1, 3):
        send(ys, yb.at[y], 8, 11, (((y + dy) % 4) * 8 + z, h))
    wait_recv(yb.at[pl.ds(0, 3)], 11)
    for i in range(8):
        zs[i] = yb[owners[i] // 8]
    zb_[zh * 8 + z] = zs[z]
    for dz, dzl in [(1, 0)] + [(d, e) for e in (4, 3, 5, 2, 6, 1, 7) for d in (1, 0)]:
        to = (z + dzl) % 8
        send(zs.at[to], zb_.at[zh * 8 + z], 9, 12, (y * 8 + to, head_at(0, dz, 0)))
    wait_recv(zb_.at[pl.ds(0, 15)], 12)
    wait_recv(gb.at[0], 20)
    from_z = owners[8] % 8
    final = (zb_[from_z].astype(F32) + zb_[8 + from_z].astype(F32)).astype(BF).astype(F32)
    out_ref[...] = jnp.where(zh == 0, final[0], final[1]).astype(BF)

    square = jnp.sum(final[0] * final[0] + final[1] * final[1], axis=-1, keepdims=True)
    product = jnp.sum(final[0] * gb[0] + final[1] * gb[1], axis=-1, keepdims=True)
    both = jnp.where(lane < 64, square, product)
    cs[...] = both
    cb[n] = both
    for dx, dc in NEAR:
        send(cs, cb.at[n], 10, 13, (r, head_at(dx, 0, dc)))
    wait_recv(cb.at[pl.ds(0, 7)], 13)
    sums = jnp.sum(cb[...], axis=0)
    score_ref[...] = jnp.broadcast_to(sums[:, 64:65] * lax.rsqrt(sums[:, 0:1] / WIDTH + EPS), (8, 128))

    wait_send(hb.at[pl.ds(0, 7)], 0)
    wait_send(hf, 15)
    wait_send(qb.at[pl.ds(0, 7)], 1)
    wait_send(qf, 16)
    wait_send(fb.at[0], 2)
    wait_send(nb.at[pl.ds(0, 7)], 3)
    wait_send(nf, 17)
    wait_send(rb.at[pl.ds(0, 7)], 4)
    wait_send(xb.at[pl.ds(0, 15)], 5)

    @pl.when(x != zz)
    def _():
        wait_send(xb.at[0], 14)
    wait_send(pb.at[pl.ds(0, 3)], 6)
    wait_send(db.at[pl.ds(0, 7)], 7)
    wait_send(yb.at[pl.ds(0, 3)], 8)
    wait_send(zb_.at[pl.ds(0, 15)], 9)
    wait_send(cb.at[pl.ds(0, 7)], 10)
    wait_send(gb.at[0], 11)
    wait_send(wgate.at[pl.ds(0, 7)], 12)
    wait_send(wup.at[pl.ds(0, 7)], 13)


def shards(
    hidden, attn_gain, q_weight, gate_weight, key_value_weight, q_gain, k_gain, out_weight,
    prompt_key_cache, prompt_value_cache, tail_key_cache, tail_value_cache, mlp_gain, mlp_gate,
    mlp_up, mlp_down, final_gain, score_weight, prompt_lengths, tail_lengths, group_prompt,
):
    vmem = pl.BlockSpec(memory_space=pltpu.VMEM)
    smem = pl.BlockSpec(memory_space=pltpu.SMEM)
    hbm = pl.BlockSpec(memory_space=pl.ANY)

    def blocks(*shape, kind=BF):
        return pltpu.VMEM(shape, kind)

    out, score = pl.pallas_call(
        kernel,
        out_shape=(jax.ShapeDtypeStruct((8, 128), BF), jax.ShapeDtypeStruct((8, 128), F32)),
        in_specs=[smem] * 3 + [vmem] * 7 + [hbm] * 11,
        out_specs=(vmem, vmem),
        scratch_shapes=[
            blocks(2048, 128), blocks(2048, 128), blocks(2048, 128), blocks(128, 2048),
            blocks(2560, 128), blocks(2560, 128),
            blocks(8, 64, 384), blocks(8, 64, 384), blocks(384, 2048),
            blocks(8, 8, 128), blocks(8, 8, 128),
            blocks(8, 128), blocks(8, 8, 128), blocks(8, 8, 128),
            blocks(8, 128), blocks(2, 8, 128),
            blocks(8, 16, 128), blocks(8, 16, 128),
            blocks(8, 16, 128), blocks(8, 16, 128),
            blocks(8, 4, 8, 128), blocks(8, 4, 8, 128),
            blocks(2, 8, 128), blocks(16, 2, 8, 128),
            blocks(4, 8, 896), blocks(4, 8, 896),
            blocks(8, 2, 8, 128), blocks(8, 2, 8, 128),
            blocks(2, 8, 128), blocks(4, 2, 8, 128),
            blocks(8, 2, 8, 128), blocks(16, 2, 8, 128),
            blocks(8, 128, kind=F32), blocks(8, 8, 128, kind=F32),
            blocks(8, 128, kind=F32), blocks(2, 8, 128, kind=F32),
            pltpu.SemaphoreType.DMA((11,)),
            pltpu.SemaphoreType.DMA((18,)),
            pltpu.SemaphoreType.DMA((23,)),
        ],
        compiler_params=pltpu.CompilerParams(
            collective_id=0, has_side_effects=True, vmem_limit_bytes=60 << 20
        ),
    )(
        prompt_lengths, tail_lengths, group_prompt,
        hidden, attn_gain.reshape(1, -1), q_gain.reshape(1, -1), k_gain.reshape(1, -1),
        mlp_gain.reshape(1, -1), final_gain.reshape(1, -1), score_weight.reshape(1, -1),
        q_weight, gate_weight, key_value_weight, out_weight,
        prompt_key_cache.reshape(-1, 128), prompt_value_cache.reshape(-1, 128),
        tail_key_cache.reshape(-1, 128), tail_value_cache.reshape(-1, 128),
        mlp_gate, mlp_up, mlp_down,
    )
    return out, score[:, 0]


def solution(mesh):
    return jax.shard_map(
        shards,
        mesh=mesh,
        in_specs=(
            P("req", "head"),
            P(),
            P(None, "head"),
            P(None, "head"),
            P(None, "head"),
            P(),
            P(),
            P("head", None),
            P("req", "head", None, None),
            P("req", "head", None, None),
            P("req", None, "head", None, None),
            P("req", None, "head", None, None),
            P(),
            P("req", "head"),
            P("req", "head"),
            P("head", None),
            P("head"),
            P("head"),
            P(),
            P(),
            P(),
        ),
        out_specs=(P("req", "head"), P("req")),
        check_vma=False,
    )
```

time: 1500 us -> 90.9 us (0.06)
  waiting for transfers between devices: 1070 us -> 0 us
  blocking collectives: 392 us -> 0 us
  Pallas kernels: 0 us -> 86.1 us
    psum x3 -> x0, waiting for transfers between devices: 639 us -> none  [the longest x1 263 us: shards(): down_total = lax.psum(down_part, 'head')]
    unnamed x5 -> x0, waiting for transfers between devices: 429 us -> none
    all_gather x4 -> x0, blocking collectives: 230 us -> none  [the longest x1 101 us: shards(): everyone = lax.all_gather(finished, 'req', axis=0, tiled=True)]
    psum x2 -> x0, blocking collectives: 146 us -> none  [the longest x1 84.3 us: shards(): lax.psum((jnp.sum(final_rows * final_rows, axis=-1), jnp.sum(final_rows *...]
    pallas_call x0 -> x1, Pallas kernels: none -> 86.1 us  [shards(): pl.pallas_call(kernel, out_shape=(jax.ShapeDtypeStruct((8, 128), BF), jax...]
    all_to_all x1 -> x0, blocking collectives: 16.2 us -> none  [shards(): lax.all_to_all(mlp_in, 'req', split_axis=1, concat_axis=0, tiled=True)]
  transfers between devices with their start and end apart: 4 -> 0, of which waited for: 4 -> 0; matrix products, arithmetic and copies ran while one was open for 0% -> 0% of each run, Pallas kernels for 0% -> 0%
where the time goes in v1:
time: 90.9 us; the launch traced here: 90.6 us
  Pallas kernels  86.1 us (95%)
  local copies, waits for them, and re-layouts  3.88 us (4%)
    pallas_call x1, Pallas kernels, shards(): pl.pallas_call(kernel, out_shape=(jax.ShapeDtypeStruct((8, 128), BF), jax...  86.1 us
    unnamed x2, local copies, waits for them, and re-layouts  2.59 us

profile of v1, /device:TPU:1, one launch (start us, length us, event | category | flops | bytes accessed | tf_op | source)
XLA Modules:
  0.0 90.6 jit_solution(6911881405448131780)
XLA Ops:
  0.6 1.4 %copy.24.tlen_ref = s32[32,4]{1,0:T(8,128)} copy(s32[32,4]{0,1:T(4,128)} %param.40) | data formatting | bytes 1024 | tf_op args[19]
  2.0 86.1 %shard_map.212 = (bf16[8,128]{1,0:T(8,128)(2,1)}, f32[8,128]{1,0:T(8,128)}) custom-call(s32[32]{0:T(128)} %plen_ref.1, s32[32,4]{1,0:T(8,128)} %copy.24.tlen_ref, s32[32]{0:T(128)} %gp_ref.1, bf16[8,128]{1,0:T(8,128)(2,1)} %hidden_ref.1, f32[1,2048]{1,0:T(1,128)} %bitcast.14, f32[1,128]{1,0:T(1,128)} %bitcast.16, f32[1,128]{1,0:T(1,128)} %bitcast.17, ...), custom_call_target="tpu_custom_call" | custom-call | tf_op jit(solution)/shard_map/pallas_call | solution.py:405
  88.1 1.3 %slice_reduce_fusion = f32[8]{0:T(128)} fusion(f32[8,128]{1,0:T(8,128)} %get-tuple-element.5), kind=kLoop, calls=%fused_computation | loop fusion | bytes 64 | tf_op jit(solution)/shard_map/slice | solution.py:443
  89.4 1.2 %copy.26 = bf16[8,128]{1,0:T(8,128)(2,1)} copy(bf16[8,128]{1,0:T(8,128)(2,1)} %get-tuple-element.8) | data formatting | bytes 4096

commit v2 on v1

--- a/solution.py
+++ b/solution.py
@@ -19,6 +19,11 @@
 NEAR = [(2, 1), (2, 0), (1, 1), (3, 1), (1, 0), (3, 0), (0, 1)]
 FAR = [(2, 1), (2, 0), (1, 1), (3, 1), (1, 0), (3, 0), (0, 1), (0, 0)]
 
+SPREAD = sorted(
+    ((dy, dx, dc) for dy in range(4) for dx in range(4) for dc in range(2) if dy or dx or dc),
+    key=lambda at: -(min(at[0], 4 - at[0]) + min(at[1], 4 - at[1]) + at[2] * 0.5),
+)
+
 
 def dot(a, b):
     return jnp.dot(a, b, preferred_element_type=F32)
@@ -29,27 +34,34 @@
 
 
 def kernel(
-    plen_ref, tlen_ref, gp_ref,
-    hidden_ref, again_ref, qgain_ref, kgain_ref, mgain_ref, fgain_ref, sw_ref,
+    plen_hbm, tlen_hbm, gp_hbm, hidden_hbm, again_hbm, qgain_hbm, kgain_hbm, mgain_hbm, fgain_hbm, sw_hbm,
     wq_hbm, wg_hbm, wkv_hbm, wo_hbm, pk_hbm, pv_hbm, tk_hbm, tv_hbm, mg_hbm, mu_hbm, md_hbm,
     out_ref, score_ref,
-    wq, wg, wkv, wo, kc, vc, wgate, wup, wdown,
-    hb, hf, qs, qb, qf, fs, fb, mb, mf, nb, nf, sb, rb, tb, xb, ps, pb, ds_, db, ys, yb, zs, zb_, cs, cb, gs, gb,
+    plen_ref, tlen_ref, gp_ref, again_ref, qgain_ref, kgain_ref, mgain_ref, fgain_ref, sw_ref,
+    wq, wg, wkv, wo, kc, vc, wmlp, wdown,
+    hb, hf, qs, qb, qf, fs, fb, mb, mf, nb, nf, sb, rb, tb, xb, ps, pb, ds_, db, yb, zs, zb_, cs, cb, gs, gb,
     lsem, ssem, rsem,
 ):
     r = lax.axis_index("req")
     h = lax.axis_index("head")
-    y, z = r // 8, r % 8
-    x, zh, c = h // 4, (h // 2) % 2, h % 2
-    zz, zb = z // 2, z % 2
+    y, z = lax.div(r, 8), lax.rem(r, 8)
+    x, zh, c = lax.div(h, 4), lax.rem(lax.div(h, 2), 2), lax.rem(h, 2)
+    zz, zb = lax.div(z, 2), lax.rem(z, 2)
     n = x * 2 + c
     oh = 1 - zh
 
+    def around(value, size):
+        shifted = [value] + [value + i for i in range(1, size)]
+        return [jnp.where(v >= size, v - size, v) for v in shifted]
+
+    xs, ys_, zzs, zls = around(x, 4), around(y, 4), around(zz, 4), around(z, 8)
+    zhs, cc, zbs = around(zh, 2), around(c, 2), around(zb, 2)
+
     def head_at(dx, dz, dc):
-        return ((x + dx) % 4) * 4 + ((zh + dz) % 2) * 2 + (c + dc) % 2
+        return xs[dx] * 4 + zhs[dz] * 2 + cc[dc]
 
     def near_at(dx, dc):
-        return ((x + dx) % 4) * 2 + (c + dc) % 2
+        return xs[dx] * 2 + cc[dc]
 
     def send(src, dst, phase, at, dev):
         pltpu.make_async_remote_copy(
@@ -70,49 +82,69 @@
         waiter(ref, phase, 0).wait_send()
 
     own_w = y * 2 + zb
-    local = [
-        (mg_hbm, wgate.at[own_w]), (mu_hbm, wup.at[own_w]),
-        (wq_hbm, wq), (wg_hbm, wg), (wkv_hbm, wkv),
-        (pk_hbm, kc.at[pl.ds(0, 2048)]), (tk_hbm, kc.at[pl.ds(2048, 512)]),
-        (pv_hbm, vc.at[pl.ds(0, 2048)]), (tv_hbm, vc.at[pl.ds(2048, 512)]),
-        (wo_hbm, wo), (md_hbm, wdown),
-    ]
-    copies = [pltpu.make_async_copy(s, d, lsem.at[i]) for i, (s, d) in enumerate(local)]
-    for cp in copies:
-        cp.start()
-
+    hidden_copy = pltpu.make_async_copy(hidden_hbm, hb.at[n], lsem.at[0])
+    hidden_copy.start()
     bar = pltpu.get_barrier_semaphore()
 
     def greet(dev):
         pl.semaphore_signal(bar, inc=1, device_id=dev, device_id_type=MESH)
 
-    for dzl in range(1, 8):
-        for dz in (1, 0):
-            greet((y * 8 + (z + dzl) % 8, head_at(0, dz, 0)))
+    for dx, dc in FAR:
+        greet((r, head_at(dx, 1, dc)))
     for dzz in (2, 1, 3, 0):
         for dz in (1, 0):
             for dc in (1, 0):
-                dev = (y * 8 + ((zz + dzz) % 4) * 2 + zb, zz * 4 + ((zh + dz) % 2) * 2 + (c + dc) % 2)
+                dev = (y * 8 + zzs[dzz] * 2 + zb, zz * 4 + zhs[dz] * 2 + cc[dc])
                 if dzz == 0 and dz == 0 and dc == 0:
                     @pl.when(x != zz)
                     def _():
                         greet(dev)
                 else:
                     greet(dev)
-    for dx, dc in FAR:
-        greet((r, head_at(dx, 1, dc)))
+    for dzl in (4, 3, 5, 2, 6, 1, 7):
+        for dz in (1, 0):
+            greet((y * 8 + zls[dzl], head_at(0, dz, 0)))
     for dx, dc in NEAR:
         greet((r, head_at(dx, 0, dc)))
     for dy in (2, 1, 3):
         for dzb in (1, 0):
-            greet((((y + dy) % 4) * 8 + zz * 2 + (zb + dzb) % 2, h))
-
-    hb[n] = hidden_ref[...]
+            greet((ys_[dy] * 8 + zz * 2 + zbs[dzb], h))
+
+    local = [
+        (mg_hbm, wmlp.at[own_w, :, pl.ds(0, 384)]), (mu_hbm, wmlp.at[own_w, :, pl.ds(384, 384)]),
+        (fgain_hbm, fgain_ref), (sw_hbm, sw_ref), (plen_hbm, plen_ref), (tlen_hbm, tlen_ref), (gp_hbm, gp_ref),
+        (again_hbm, again_ref), (wq_hbm, wq), (qgain_hbm, qgain_ref), (kgain_hbm, kgain_ref),
+        (wg_hbm, wg), (wkv_hbm, wkv),
+        (pk_hbm, kc.at[pl.ds(0, 2048)]), (tk_hbm, kc.at[pl.ds(2048, 512)]),
+        (pv_hbm, vc.at[pl.ds(0, 2048)]), (tv_hbm, vc.at[pl.ds(2048, 512)]),
+        (wo_hbm, wo), (mgain_hbm, mgain_ref), (md_hbm, wdown),
+    ]
+    copies = [pltpu.make_async_copy(s, d, lsem.at[i + 1]) for i, (s, d) in enumerate(local)]
+    for cp in copies:
+        cp.start()
+    hidden_copy.wait()
+    pl.semaphore_wait(bar, 50 + jnp.where(x != zz, 1, 0))
+
+    for dx, dc in FAR:
+        send(hb.at[n], hf.at[n], 15, 1, (r, head_at(dx, 1, dc)))
+    for dx, dc in NEAR:
+        send(hb.at[n], hb.at[n], 0, 0, (r, head_at(dx, 0, dc)))
+
+    copies[0].wait()
+    copies[1].wait()
+    for dy in (2, 1, 3, 0):
+        for dzb in (1, 0):
+            if dy or dzb:
+                send(wmlp.at[own_w], wmlp.at[own_w], 12, 21, (ys_[dy] * 8 + zz * 2 + zbs[dzb], h))
+    for i in range(2, 20):
+        copies[i].wait()
     gs[...] = jnp.broadcast_to(fgain_ref[...] * sw_ref[...], (8, 128))
+    gb[zh] = gs[...]
+    send(gs, gb.at[zh], 11, 20, (r, head_at(0, 1, 0)))
 
     prompt = gp_ref[r]
     plen = plen_ref[prompt]
-    tails = [tlen_ref[prompt, i] for i in range(4)]
+    tails = [tlen_ref[i, prompt] for i in range(4)]
 
     def find(g, found):
         value = gp_ref[g]
@@ -136,27 +168,6 @@
     def normed_rotated(value, gain):
         value = value * lax.rsqrt(jnp.mean(value * value, axis=-1, keepdims=True) + EPS) * gain
         return value * cosine + pltpu.roll(value, 64, 1) * sine
-
-    pl.semaphore_wait(bar, 50 + jnp.where(x != zz, 1, 0))
-
-    for dx, dc in FAR:
-        send(hidden_ref, hf.at[n], 15, 1, (r, head_at(dx, 1, dc)))
-    for dx, dc in NEAR:
-        send(hidden_ref, hb.at[n], 0, 0, (r, head_at(dx, 0, dc)))
-    send(gs, gb.at[zh], 11, 20, (r, head_at(0, 1, 0)))
-    gb[zh] = gs[...]
-
-    copies[0].wait()
-    copies[1].wait()
-    for dy in (2, 1, 3, 0):
-        for dzb in (1, 0):
-            if dy or dzb:
-                dev = (((y + dy) % 4) * 8 + zz * 2 + (zb + dzb) % 2, h)
-                send(wgate.at[own_w], wgate.at[own_w], 12, 21, dev)
-                send(wup.at[own_w], wup.at[own_w], 13, 22, dev)
-
-    for i in range(2, 11):
-        copies[i].wait()
 
     def features(half, at):
         place = at * 4 + half * 2
@@ -268,11 +279,11 @@
     first = jnp.where(zh == 0, 1.0, 0.0)
 
     def hidden_at(place):
-        both = jnp.where(x // 2 == 0, hb[place].astype(F32), hf[place].astype(F32))
+        both = jnp.where(x < 2, hb[place].astype(F32), hf[place].astype(F32))
         return both * first
 
-    tb[0] = (sums[0] + hidden_at(4 * c + x % 2)).astype(BF)
-    tb[1] = (sums[1] + hidden_at(4 * c + 2 + x % 2)).astype(BF)
+    tb[0] = (sums[0] + hidden_at(4 * c + lax.rem(x, 2))).astype(BF)
+    tb[1] = (sums[1] + hidden_at(4 * c + 2 + lax.rem(x, 2))).astype(BF)
     residual = [sums[2] + hb[n].astype(F32) * first, sums[3] + hf[n].astype(F32) * first]
 
     slot = (zh * 4 + zz) * 2 + c
@@ -307,19 +318,16 @@
     high = square.astype(BF).astype(F32)
     lanes = lax.broadcasted_iota(jnp.int32, (32, 128), 1)
     square = jnp.where(lanes < 64, high, square - high)
-    wait_recv(wgate.at[pl.ds(0, 7)], 21)
-    wait_recv(wup.at[pl.ds(0, 7)], 22)
-    gate_part = dot(mlp_in, wgate[...].reshape(512, 384))
-    up_part = dot(mlp_in, wup[...].reshape(512, 384))
+    wait_recv(wmlp.at[pl.ds(0, 7)], 21)
+    both = dot(mlp_in, wmlp[...].reshape(512, 768))
 
     for i in range(4):
         rows = slice(i * 8, i * 8 + 8)
-        ps[i, :, 0:384] = gate_part[rows].astype(BF)
-        ps[i, :, 384:768] = up_part[rows].astype(BF)
+        ps[i, :, 0:768] = both[rows].astype(BF)
         ps[i, :, 768:896] = square[rows].astype(BF)
     pb[zz] = ps[zz]
     for dzz in (2, 1, 3):
-        to = (zz + dzz) % 4
+        to = zzs[dzz]
         send(ps.at[to], pb.at[zz], 6, 9, (y * 8 + 2 * to + zb, h))
     wait_recv(pb.at[pl.ds(0, 3)], 9)
     sums = jnp.sum(pb[...].astype(F32), axis=0)
@@ -331,28 +339,24 @@
         px, pc = place // 2, place % 2
         for j, block in enumerate((4 * px + pc, 4 * px + 2 + pc)):
             ds_[place, j] = down[:, block * 128:(block + 1) * 128].astype(BF)
-    db[n] = ds_[n]
-    for dx, dc in NEAR:
-        send(ds_.at[near_at(dx, dc)], db.at[n], 7, 10, (r, head_at(dx, 0, dc)))
-    wait_recv(db.at[pl.ds(0, 7)], 10)
-    sums = jnp.sum(db[...].astype(F32), axis=0)
     for j in range(2):
-        value = (sums[j] + residual[j]).astype(BF)
-        ys[j] = value
-        yb[y, j] = value
-
-    for dy in (2, 1, 3):
-        send(ys, yb.at[y], 8, 11, (((y + dy) % 4) * 8 + z, h))
-    wait_recv(yb.at[pl.ds(0, 3)], 11)
+        ds_[n, j] = (ds_[n, j].astype(F32) + residual[j]).astype(BF)
+    db[y * 8 + n] = ds_[n]
+    for dy, dx, dc in SPREAD:
+        send(ds_.at[near_at(dx, dc)], db.at[y * 8 + n], 7, 10, (ys_[dy] * 8 + z, head_at(dx, 0, dc)))
+    wait_recv(db.at[pl.ds(0, 31)], 10)
+    for i in range(4):
+        yb[i] = jnp.sum(db[pl.ds(i * 8, 8)].astype(F32), axis=0).astype(BF)
+
     for i in range(8):
-        zs[i] = yb[owners[i] // 8]
+        zs[i] = yb[lax.div(owners[i], 8)]
     zb_[zh * 8 + z] = zs[z]
     for dz, dzl in [(1, 0)] + [(d, e) for e in (4, 3, 5, 2, 6, 1, 7) for d in (1, 0)]:
-        to = (z + dzl) % 8
+        to = zls[dzl]
         send(zs.at[to], zb_.at[zh * 8 + z], 9, 12, (y * 8 + to, head_at(0, dz, 0)))
     wait_recv(zb_.at[pl.ds(0, 15)], 12)
     wait_recv(gb.at[0], 20)
-    from_z = owners[8] % 8
+    from_z = lax.rem(owners[8], 8)
     final = (zb_[from_z].astype(F32) + zb_[8 + from_z].astype(F32)).astype(BF).astype(F32)
     out_ref[...] = jnp.where(zh == 0, final[0], final[1]).astype(BF)
 
@@ -381,13 +385,11 @@
     def _():
         wait_send(xb.at[0], 14)
     wait_send(pb.at[pl.ds(0, 3)], 6)
-    wait_send(db.at[pl.ds(0, 7)], 7)
-    wait_send(yb.at[pl.ds(0, 3)], 8)
+    wait_send(db.at[pl.ds(0, 31)], 7)
     wait_send(zb_.at[pl.ds(0, 15)], 9)
     wait_send(cb.at[pl.ds(0, 7)], 10)
     wait_send(gb.at[0], 11)
-    wait_send(wgate.at[pl.ds(0, 7)], 12)
-    wait_send(wup.at[pl.ds(0, 7)], 13)
+    wait_send(wmlp.at[pl.ds(0, 7)], 12)
 
 
 def shards(
@@ -396,7 +398,6 @@
     mlp_up, mlp_down, final_gain, score_weight, prompt_lengths, tail_lengths, group_prompt,
 ):
     vmem = pl.BlockSpec(memory_space=pltpu.VMEM)
-    smem = pl.BlockSpec(memory_space=pltpu.SMEM)
     hbm = pl.BlockSpec(memory_space=pl.ANY)
 
     def blocks(*shape, kind=BF):
@@ -405,12 +406,15 @@
     out, score = pl.pallas_call(
         kernel,
         out_shape=(jax.ShapeDtypeStruct((8, 128), BF), jax.ShapeDtypeStruct((8, 128), F32)),
-        in_specs=[smem] * 3 + [vmem] * 7 + [hbm] * 11,
+        in_specs=[hbm] * 21,
         out_specs=(vmem, vmem),
         scratch_shapes=[
+            pltpu.SMEM((32,), jnp.int32), pltpu.SMEM((4, 32), jnp.int32), pltpu.SMEM((32,), jnp.int32),
+            blocks(1, 2048, kind=F32), blocks(1, 128, kind=F32), blocks(1, 128, kind=F32),
+            blocks(1, 2048, kind=F32), blocks(1, 128, kind=F32), blocks(1, 128, kind=F32),
             blocks(2048, 128), blocks(2048, 128), blocks(2048, 128), blocks(128, 2048),
             blocks(2560, 128), blocks(2560, 128),
-            blocks(8, 64, 384), blocks(8, 64, 384), blocks(384, 2048),
+            blocks(8, 64, 768), blocks(384, 2048),
             blocks(8, 8, 128), blocks(8, 8, 128),
             blocks(8, 128), blocks(8, 8, 128), blocks(8, 8, 128),
             blocks(8, 128), blocks(2, 8, 128),
@@ -419,12 +423,12 @@
             blocks(8, 4, 8, 128), blocks(8, 4, 8, 128),
             blocks(2, 8, 128), blocks(16, 2, 8, 128),
             blocks(4, 8, 896), blocks(4, 8, 896),
-            blocks(8, 2, 8, 128), blocks(8, 2, 8, 128),
-            blocks(2, 8, 128), blocks(4, 2, 8, 128),
+            blocks(8, 2, 8, 128), blocks(32, 2, 8, 128),
+            blocks(4, 2, 8, 128),
             blocks(8, 2, 8, 128), blocks(16, 2, 8, 128),
             blocks(8, 128, kind=F32), blocks(8, 8, 128, kind=F32),
             blocks(8, 128, kind=F32), blocks(2, 8, 128, kind=F32),
-            pltpu.SemaphoreType.DMA((11,)),
+            pltpu.SemaphoreType.DMA((21,)),
             pltpu.SemaphoreType.DMA((18,)),
             pltpu.SemaphoreType.DMA((23,)),
         ],
@@ -432,7 +436,7 @@
             collective_id=0, has_side_effects=True, vmem_limit_bytes=60 << 20
         ),
     )(
-        prompt_lengths, tail_lengths, group_prompt,
+        prompt_lengths, tail_lengths.T, group_prompt,
         hidden, attn_gain.reshape(1, -1), q_gain.reshape(1, -1), k_gain.reshape(1, -1),
         mlp_gain.reshape(1, -1), final_gain.reshape(1, -1), score_weight.reshape(1, -1),
         q_weight, gate_weight, key_value_weight, out_weight,

time: 90.9 us -> 86.3 us (0.949)
  Pallas kernels: 86.1 us -> 82.8 us
  local copies, waits for them, and re-layouts: 3.88 us -> 2.56 us
    pallas_call x1, Pallas kernels: 86.1 us -> 82.8 us  [shards(): pl.pallas_call(kernel, out_shape=(jax.ShapeDtypeStruct((8, 128), BF), jax...]
    unnamed x2 -> x1, local copies, waits for them, and re-layouts: 2.59 us -> 1.25 us
where the time goes in v2:
time: 86.3 us; the launch traced here: 86.1 us
  Pallas kernels  82.8 us (96%)
  local copies, waits for them, and re-layouts  2.56 us (3%)
    pallas_call x1, Pallas kernels, shards(): pl.pallas_call(kernel, out_shape=(jax.ShapeDtypeStruct((8, 128), BF), jax...  82.8 us

profile of v2, /device:TPU:1, one launch (start us, length us, event | category | flops | bytes accessed | tf_op | source)
XLA Modules:
  0.0 86.1 jit_solution(17100166353174286965)
XLA Ops:
  0.6 82.8 %shard_map.212 = (bf16[8,128]{1,0:T(8,128)(2,1)}, f32[8,128]{1,0:T(8,128)}) custom-call(s32[32]{0:T(128)} %plen_hbm.1, s32[4,32]{1,0:T(4,128)} %bitcast.17, s32[32]{0:T(128)} %gp_hbm.1, bf16[8,128]{1,0:T(8,128)(2,1)} %hidden_hbm.1, f32[1,2048]{1,0:T(1,128)} %bitcast.15, f32[1,128]{1,0:T(1,128)} %bitcast.18, f32[1,128]{1,0:T(1,128)} %bitcast.19, ...), custom_call_target="tpu_custom_call" | custom-call | tf_op jit(solution)/shard_map/pallas_call | solution.py:406
  83.5 1.3 %slice_reduce_fusion = f32[8]{0:T(128)} fusion(f32[8,128]{1,0:T(8,128)} %get-tuple-element.5), kind=kLoop, calls=%fused_computation | loop fusion | bytes 64 | tf_op jit(solution)/shard_map/slice | solution.py:447
  84.8 1.2 %copy.24 = bf16[8,128]{1,0:T(8,128)(2,1)} copy(bf16[8,128]{1,0:T(8,128)(2,1)} %get-tuple-element.8) | data formatting | bytes 4096

commit v3 on v2

--- a/solution.py
+++ b/solution.py
@@ -38,15 +38,15 @@
     wq_hbm, wg_hbm, wkv_hbm, wo_hbm, pk_hbm, pv_hbm, tk_hbm, tv_hbm, mg_hbm, mu_hbm, md_hbm,
     out_ref, score_ref,
     plen_ref, tlen_ref, gp_ref, again_ref, qgain_ref, kgain_ref, mgain_ref, fgain_ref, sw_ref,
-    wq, wg, wkv, wo, kc, vc, wmlp, wdown,
+    wq, wg, wkv, wo, kc, vc, wmlp, wfar, wdown,
     hb, hf, qs, qb, qf, fs, fb, mb, mf, nb, nf, sb, rb, tb, xb, ps, pb, ds_, db, yb, zs, zb_, cs, cb, gs, gb,
-    lsem, ssem, rsem,
+    lsem, ssem, rsem, qsem,
 ):
     r = lax.axis_index("req")
     h = lax.axis_index("head")
     y, z = lax.div(r, 8), lax.rem(r, 8)
     x, zh, c = lax.div(h, 4), lax.rem(lax.div(h, 2), 2), lax.rem(h, 2)
-    zz, zb = lax.div(z, 2), lax.rem(z, 2)
+    zt, zq = lax.div(z, 4), lax.rem(z, 4)
     n = x * 2 + c
     oh = 1 - zh
 
@@ -54,8 +54,10 @@
         shifted = [value] + [value + i for i in range(1, size)]
         return [jnp.where(v >= size, v - size, v) for v in shifted]
 
-    xs, ys_, zzs, zls = around(x, 4), around(y, 4), around(zz, 4), around(z, 8)
-    zhs, cc, zbs = around(zh, 2), around(c, 2), around(zb, 2)
+    xs, ys_, zqs, zls = around(x, 4), around(y, 4), around(zq, 4), around(z, 8)
+    zhs, cc = around(zh, 2), around(c, 2)
+    own_w, other_w = y * 2 + zt, y * 2 + 1 - zt
+    across = (y * 8 + (1 - zt) * 4 + zq, h)
 
     def head_at(dx, dz, dc):
         return xs[dx] * 4 + zhs[dz] * 2 + cc[dc]
@@ -81,7 +83,6 @@
     def wait_send(ref, phase):
         waiter(ref, phase, 0).wait_send()
 
-    own_w = y * 2 + zb
     hidden_copy = pltpu.make_async_copy(hidden_hbm, hb.at[n], lsem.at[0])
     hidden_copy.start()
     bar = pltpu.get_barrier_semaphore()
@@ -91,24 +92,13 @@
 
     for dx, dc in FAR:
         greet((r, head_at(dx, 1, dc)))
-    for dzz in (2, 1, 3, 0):
-        for dz in (1, 0):
-            for dc in (1, 0):
-                dev = (y * 8 + zzs[dzz] * 2 + zb, zz * 4 + zhs[dz] * 2 + cc[dc])
-                if dzz == 0 and dz == 0 and dc == 0:
-                    @pl.when(x != zz)
-                    def _():
-                        greet(dev)
-                else:
-                    greet(dev)
-    for dzl in (4, 3, 5, 2, 6, 1, 7):
-        for dz in (1, 0):
-            greet((y * 8 + zls[dzl], head_at(0, dz, 0)))
+    greet(across)
+    for dzq in (2, 3, 1):
+        greet((y * 8 + zt * 4 + zqs[dzq], h))
+    for dy in (2, 1, 3):
+        greet((ys_[dy] * 8 + z, h))
     for dx, dc in NEAR:
         greet((r, head_at(dx, 0, dc)))
-    for dy in (2, 1, 3):
-        for dzb in (1, 0):
-            greet((ys_[dy] * 8 + zz * 2 + zbs[dzb], h))
 
     local = [
         (mg_hbm, wmlp.at[own_w, :, pl.ds(0, 384)]), (mu_hbm, wmlp.at[own_w, :, pl.ds(384, 384)]),
@@ -123,7 +113,7 @@
     for cp in copies:
         cp.start()
     hidden_copy.wait()
-    pl.semaphore_wait(bar, 50 + jnp.where(x != zz, 1, 0))
+    pl.semaphore_wait(bar, 22)
 
     for dx, dc in FAR:
         send(hb.at[n], hf.at[n], 15, 1, (r, head_at(dx, 1, dc)))
@@ -132,10 +122,11 @@
 
     copies[0].wait()
     copies[1].wait()
-    for dy in (2, 1, 3, 0):
-        for dzb in (1, 0):
-            if dy or dzb:
-                send(wmlp.at[own_w], wmlp.at[own_w], 12, 21, (ys_[dy] * 8 + zz * 2 + zbs[dzb], h))
+    send(wmlp.at[own_w], wfar, 13, 22, across)
+    for dy in (2, 1, 3):
+        send(wmlp.at[own_w], wmlp.at[own_w], 12, 21, (ys_[dy] * 8 + z, h))
+    for dzq in (2, 3, 1):
+        pl.semaphore_signal(qsem, inc=1, device_id=(y * 8 + zt * 4 + zqs[dzq], h), device_id_type=MESH)
     for i in range(2, 20):
         copies[i].wait()
     gs[...] = jnp.broadcast_to(fgain_ref[...] * sw_ref[...], (8, 128))
@@ -205,6 +196,12 @@
     for dx, dc in NEAR:
         send(qs, qb.at[n], 1, 2, (r, head_at(dx, 0, dc)))
 
+    wait_recv(wfar, 22)
+    for dy in (2, 1, 3):
+        send(wfar, wmlp.at[other_w], 8, 11, (ys_[dy] * 8 + z, h))
+    kept = pltpu.make_async_copy(wfar, wmlp.at[other_w], lsem.at[21])
+    kept.start()
+
     for scaled, offset in rest:
         g_acc = g_acc + dot(scaled, wg[pl.ds(offset, 256), :])
         kv_acc = kv_acc + dot(scaled, wkv[pl.ds(offset, 256), :])
@@ -266,11 +263,20 @@
     total = total + sums[8:, 0:1] + sums[8:, 64:65]
     gated = (numer / total * gate).astype(BF)
 
+    def quarter(low, high, odd):
+        low = jnp.where(odd == 0, low, pltpu.roll(low, 64, 1))
+        high = jnp.where(odd == 0, pltpu.roll(high, 64, 1), high)
+        return jnp.where(lane < 64, low, high)
+
     mixed = dot(gated, wo[...])
     for place in range(8):
         px, pc = place // 2, place % 2
-        for j, block in enumerate((8 * pc + px, 8 * pc + 4 + px, 4 * px + pc, 4 * px + 2 + pc)):
-            sb[place, j] = mixed[:, block * 128:(block + 1) * 128].astype(BF)
+        for j in range(2):
+            at = (2 * pc + j) * 512 + px * 64
+            pieces = [mixed[:, at:at + 64], mixed[:, at + 256:at + 320]]
+            sb[place, j] = jnp.concatenate(pieces, axis=1).astype(BF)
+            block = 4 * px + 2 * j + pc
+            sb[place, 2 + j] = mixed[:, block * 128:(block + 1) * 128].astype(BF)
     rb[n] = sb[n]
     for dx, dc in NEAR:
         send(sb.at[near_at(dx, dc)], rb.at[n], 4, 7, (r, head_at(dx, 0, dc)))
@@ -278,28 +284,34 @@
     sums = jnp.sum(rb[...].astype(F32), axis=0)
     first = jnp.where(zh == 0, 1.0, 0.0)
 
-    def hidden_at(place):
-        both = jnp.where(x < 2, hb[place].astype(F32), hf[place].astype(F32))
-        return both * first
-
-    tb[0] = (sums[0] + hidden_at(4 * c + lax.rem(x, 2))).astype(BF)
-    tb[1] = (sums[1] + hidden_at(4 * c + 2 + lax.rem(x, 2))).astype(BF)
+    for j in range(2):
+        place = (2 * c + j) * 2 + lax.div(x, 2)
+        tb[j] = (sums[j] + quarter(hb[place].astype(F32), hf[place].astype(F32), lax.rem(x, 2)) * first).astype(BF)
     residual = [sums[2] + hb[n].astype(F32) * first, sums[3] + hf[n].astype(F32) * first]
 
-    slot = (zh * 4 + zz) * 2 + c
-    target = y * 8 + 2 * x + zb
+    slot = (zh * 4 + zq) * 2 + c
+    target = y * 8 + zt * 4 + x
+    pl.semaphore_wait(qsem, 3)
     for dz in (1, 0):
         for dx, dc in FAR:
             if dz or dx or dc:
                 send(tb, xb.at[slot], 5, 8, (target, head_at(dx, dz, dc)))
 
-    @pl.when(x != zz)
+    @pl.when(x != zq)
     def _():
         send(tb, xb.at[slot], 14, 8, (target, h))
 
         wait_recv(xb, 8)
 
-    @pl.when(x == zz)
+    gains = []
+    for fy in range(4):
+        pair = []
+        for i in range(2):
+            offset = pl.multiple_of((fy * 4 + 2 * i + lax.div(zq, 2)) * 128, 128)
+            pair.append(jnp.broadcast_to(mgain_ref[:, pl.ds(offset, 128)], (8, 128)))
+        gains.append(quarter(*pair, lax.rem(zq, 2))[0:1])
+
+    @pl.when(x == zq)
     def _():
         xb[slot] = tb[...]
         wait_recv(xb.at[pl.ds(0, 15)], 8)
@@ -311,24 +323,25 @@
     for fy in range(4):
         block = jnp.concatenate([attended[i * 2 + fy // 2, fy % 2] for i in range(4)], axis=0)
         squares = squares + block * block
-        offset = pl.multiple_of((fy * 4 + zz) * 128, 128)
-        parts.append((block * mgain_ref[:, pl.ds(offset, 128)]).astype(BF))
+        parts.append((block * gains[fy]).astype(BF))
     mlp_in = jnp.concatenate(parts, axis=1)
     square = jnp.sum(squares, axis=-1, keepdims=True)
     high = square.astype(BF).astype(F32)
     lanes = lax.broadcasted_iota(jnp.int32, (32, 128), 1)
     square = jnp.where(lanes < 64, high, square - high)
-    wait_recv(wmlp.at[pl.ds(0, 7)], 21)
+    wait_recv(wmlp.at[pl.ds(0, 3)], 21)
+    wait_recv(wmlp.at[pl.ds(0, 3)], 11)
+    kept.wait()
     both = dot(mlp_in, wmlp[...].reshape(512, 768))
 
     for i in range(4):
         rows = slice(i * 8, i * 8 + 8)
         ps[i, :, 0:768] = both[rows].astype(BF)
         ps[i, :, 768:896] = square[rows].astype(BF)
-    pb[zz] = ps[zz]
-    for dzz in (2, 1, 3):
-        to = zzs[dzz]
-        send(ps.at[to], pb.at[zz], 6, 9, (y * 8 + 2 * to + zb, h))
+    pb[zq] = ps[zq]
+    for dzq in (2, 3, 1):
+        to = zqs[dzq]
+        send(ps.at[to], pb.at[zq], 6, 9, (y * 8 + zt * 4 + to, h))
     wait_recv(pb.at[pl.ds(0, 3)], 9)
     sums = jnp.sum(pb[...].astype(F32), axis=0)
     scale = lax.rsqrt((sums[:, 768:769] + sums[:, 832:833]) / WIDTH + EPS)
@@ -360,16 +373,15 @@
     final = (zb_[from_z].astype(F32) + zb_[8 + from_z].astype(F32)).astype(BF).astype(F32)
     out_ref[...] = jnp.where(zh == 0, final[0], final[1]).astype(BF)
 
-    square = jnp.sum(final[0] * final[0] + final[1] * final[1], axis=-1, keepdims=True)
-    product = jnp.sum(final[0] * gb[0] + final[1] * gb[1], axis=-1, keepdims=True)
-    both = jnp.where(lane < 64, square, product)
-    cs[...] = both
-    cb[n] = both
+    cs[0] = final[0] * final[0] + final[1] * final[1]
+    cs[1] = final[0] * gb[0] + final[1] * gb[1]
+    cb[n] = cs[...]
     for dx, dc in NEAR:
         send(cs, cb.at[n], 10, 13, (r, head_at(dx, 0, dc)))
     wait_recv(cb.at[pl.ds(0, 7)], 13)
-    sums = jnp.sum(cb[...], axis=0)
-    score_ref[...] = jnp.broadcast_to(sums[:, 64:65] * lax.rsqrt(sums[:, 0:1] / WIDTH + EPS), (8, 128))
+    sums = jnp.sum(jnp.sum(cb[...], axis=0), axis=-1, keepdims=True)
+    score = sums[1] * lax.rsqrt(sums[0] / WIDTH + EPS)
+    score_ref[...] = jnp.sum(jnp.where(row == lane, score, 0.0), axis=0, keepdims=True)
 
     wait_send(hb.at[pl.ds(0, 7)], 0)
     wait_send(hf, 15)
@@ -381,7 +393,7 @@
     wait_send(rb.at[pl.ds(0, 7)], 4)
     wait_send(xb.at[pl.ds(0, 15)], 5)
 
-    @pl.when(x != zz)
+    @pl.when(x != zq)
     def _():
         wait_send(xb.at[0], 14)
     wait_send(pb.at[pl.ds(0, 3)], 6)
@@ -389,7 +401,14 @@
     wait_send(zb_.at[pl.ds(0, 15)], 9)
     wait_send(cb.at[pl.ds(0, 7)], 10)
     wait_send(gb.at[0], 11)
-    wait_send(wmlp.at[pl.ds(0, 7)], 12)
+    wait_send(wmlp.at[pl.ds(0, 3)], 12)
+    wait_send(wmlp.at[0], 13)
+    wait_send(wmlp.at[pl.ds(0, 3)], 8)
+
+
+def hand_over(out_from, score_from, out_ref, score_ref):
+    out_ref[...] = out_from[...]
+    score_ref[...] = score_from[:, 0:8]
 
 
 def shards(
@@ -405,7 +424,7 @@
 
     out, score = pl.pallas_call(
         kernel,
-        out_shape=(jax.ShapeDtypeStruct((8, 128), BF), jax.ShapeDtypeStruct((8, 128), F32)),
+        out_shape=(jax.ShapeDtypeStruct((8, 128), BF), jax.ShapeDtypeStruct((1, 128), F32)),
         in_specs=[hbm] * 21,
         out_specs=(vmem, vmem),
         scratch_shapes=[
@@ -414,7 +433,7 @@
             blocks(1, 2048, kind=F32), blocks(1, 128, kind=F32), blocks(1, 128, kind=F32),
             blocks(2048, 128), blocks(2048, 128), blocks(2048, 128), blocks(128, 2048),
             blocks(2560, 128), blocks(2560, 128),
-            blocks(8, 64, 768), blocks(384, 2048),
+            blocks(8, 64, 768), blocks(64, 768), blocks(384, 2048),
             blocks(8, 8, 128), blocks(8, 8, 128),
             blocks(8, 128), blocks(8, 8, 128), blocks(8, 8, 128),
             blocks(8, 128), blocks(2, 8, 128),
@@ -426,11 +445,12 @@
             blocks(8, 2, 8, 128), blocks(32, 2, 8, 128),
             blocks(4, 2, 8, 128),
             blocks(8, 2, 8, 128), blocks(16, 2, 8, 128),
-            blocks(8, 128, kind=F32), blocks(8, 8, 128, kind=F32),
+            blocks(2, 8, 128, kind=F32), blocks(8, 2, 8, 128, kind=F32),
             blocks(8, 128, kind=F32), blocks(2, 8, 128, kind=F32),
-            pltpu.SemaphoreType.DMA((21,)),
+            pltpu.SemaphoreType.DMA((22,)),
             pltpu.SemaphoreType.DMA((18,)),
             pltpu.SemaphoreType.DMA((23,)),
+            pltpu.SemaphoreType.REGULAR,
         ],
         compiler_params=pltpu.CompilerParams(
             collective_id=0, has_side_effects=True, vmem_limit_bytes=60 << 20
@@ -444,7 +464,13 @@
         tail_key_cache.reshape(-1, 128), tail_value_cache.reshape(-1, 128),
         mlp_gate, mlp_up, mlp_down,
     )
-    return out, score[:, 0]
+    out, score = pl.pallas_call(
+        hand_over,
+        out_shape=(jax.ShapeDtypeStruct((8, 128), BF), jax.ShapeDtypeStruct((1, 8), F32)),
+        in_specs=[vmem] * 2,
+        out_specs=(vmem, vmem),
+    )(out, score)
+    return out, score[0]
 
 
 def solution(mesh):

time: 86.3 us -> 83.6 us (0.969)
  local copies, waits for them, and re-layouts: 2.56 us -> 0 us
    slice x1 -> x0, local copies, waits for them, and re-layouts: 1.31 us -> none  [shards(): return (out, score[:, 0])]
    pallas_call x1, Pallas kernels: 82.8 us -> 81.5 us  [shards(): pl.pallas_call(kernel, out_shape=(jax.ShapeDtypeStruct((8, 128), BF), jax...]
    pallas_call x0 -> x1, Pallas kernels: none -> 1.25 us  [shards(): pl.pallas_call(hand_over, out_shape=(jax.ShapeDtypeStruct((8, 128), BF),...]
    unnamed x1 -> x0, local copies, waits for them, and re-layouts: 1.25 us -> none
where the time goes in v3:
time: 83.6 us; the launch traced here: 83.4 us
  Pallas kernels  82.8 us (99%)
    pallas_call x1, Pallas kernels, shards(): pl.pallas_call(kernel, out_shape=(jax.ShapeDtypeStruct((8, 128), BF), jax...  81.5 us

profile of v3, /device:TPU:1, one launch (start us, length us, event | category | flops | bytes accessed | tf_op | source)
XLA Modules:
  0.0 83.4 jit_solution(3977430459948541688)
XLA Ops:
  0.6 81.5 %shard_map.212 = (bf16[8,128]{1,0:T(8,128)(2,1)}, f32[1,128]{1,0:T(1,128)}) custom-call(s32[32]{0:T(128)} %plen_hbm.1, s32[4,32]{1,0:T(4,128)} %bitcast.18, s32[32]{0:T(128)} %gp_hbm.1, bf16[8,128]{1,0:T(8,128)(2,1)} %hidden_hbm.1, f32[1,2048]{1,0:T(1,128)} %bitcast.16, f32[1,128]{1,0:T(1,128)} %bitcast.19, f32[1,128]{1,0:T(1,128)} %bitcast.20, ...), custom_call_target="tpu_custom_call" | custom-call | tf_op jit(solution)/shard_map/pallas_call | solution.py:425
  82.2 1.3 %shard_map.213 = (bf16[8,128]{1,0:T(8,128)(2,1)}, f32[1,8]{1,0:T(1,128)}) custom-call(bf16[8,128]{1,0:T(8,128)(2,1)} %get-tuple-element.6.out_from, f32[1,128]{1,0:T(1,128)} %get-tuple-element.7.score_from), custom_call_target="tpu_custom_call" | custom-call | tf_op jit(solution)/shard_map/pallas_call | solution.py:467

commit v4 on v3

--- a/solution.py
+++ b/solution.py
@@ -1,4 +1,3 @@
-import functools
 import math
 
 import jax
@@ -23,6 +22,8 @@
     ((dy, dx, dc) for dy in range(4) for dx in range(4) for dc in range(2) if dy or dx or dc),
     key=lambda at: -(min(at[0], 4 - at[0]) + min(at[1], 4 - at[1]) + at[2] * 0.5),
 )
+
+RING = [(1, 0), (1, 1), (1, 7), (1, 2), (1, 6), (0, 4), (1, 3), (1, 5), (0, 3), (0, 5), (1, 4), (0, 2), (0, 6), (0, 1), (0, 7)]
 
 
 def dot(a, b):
@@ -364,7 +365,7 @@
     for i in range(8):
         zs[i] = yb[lax.div(owners[i], 8)]
     zb_[zh * 8 + z] = zs[z]
-    for dz, dzl in [(1, 0)] + [(d, e) for e in (4, 3, 5, 2, 6, 1, 7) for d in (1, 0)]:
+    for dz, dzl in RING:
         to = zls[dzl]
         send(zs.at[to], zb_.at[zh * 8 + z], 9, 12, (y * 8 + to, head_at(0, dz, 0)))
     wait_recv(zb_.at[pl.ds(0, 15)], 12)
@@ -406,11 +407,6 @@
     wait_send(wmlp.at[pl.ds(0, 3)], 8)
 
 
-def hand_over(out_from, score_from, out_ref, score_ref):
-    out_ref[...] = out_from[...]
-    score_ref[...] = score_from[:, 0:8]
-
-
 def shards(
     hidden, attn_gain, q_weight, gate_weight, key_value_weight, q_gain, k_gain, out_weight,
     prompt_key_cache, prompt_value_cache, tail_key_cache, tail_value_cache, mlp_gain, mlp_gate,
@@ -424,7 +420,7 @@
 
     out, score = pl.pallas_call(
         kernel,
-        out_shape=(jax.ShapeDtypeStruct((8, 128), BF), jax.ShapeDtypeStruct((1, 128), F32)),
+        out_shape=(pltpu.VMEM((8, 128), BF), pltpu.VMEM((1, 128), F32)),
         in_specs=[hbm] * 21,
         out_specs=(vmem, vmem),
         scratch_shapes=[
@@ -464,13 +460,7 @@
         tail_key_cache.reshape(-1, 128), tail_value_cache.reshape(-1, 128),
         mlp_gate, mlp_up, mlp_down,
     )
-    out, score = pl.pallas_call(
-        hand_over,
-        out_shape=(jax.ShapeDtypeStruct((8, 128), BF), jax.ShapeDtypeStruct((1, 8), F32)),
-        in_specs=[vmem] * 2,
-        out_specs=(vmem, vmem),
-    )(out, score)
-    return out, score[0]
+    return out, score[0, :8]
 
 
 def solution(mesh):

time: 83.6 us -> 82.9 us (level)
  Pallas kernels: 82.8 us -> 81 us
  local copies, waits for them, and re-layouts: 0 us -> 1.09 us
    pallas_call x2 -> x1, Pallas kernels: 82.8 us -> 81 us  [shards(): pl.pallas_call(kernel, out_shape=(pltpu.VMEM((8, 128), BF), pltpu.VMEM((1...]
where the time goes in v4:
time: 82.9 us; the launch traced here: 82.8 us
  Pallas kernels  81 us (98%)
  local copies, waits for them, and re-layouts  1.09 us (1%)
    pallas_call x1, Pallas kernels, shards(): pl.pallas_call(kernel, out_shape=(pltpu.VMEM((8, 128), BF), pltpu.VMEM((1...  81 us

profile of v4, /device:TPU:1, one launch (start us, length us, event | category | flops | bytes accessed | tf_op | source)
XLA Modules:
  0.0 82.8 jit_solution(10193047296464817756)
XLA Ops:
  0.6 81.0 %shard_map.212 = (bf16[8,128]{1,0:T(8,128)(2,1)S(1)}, f32[1,128]{1,0:T(1,128)S(1)}) custom-call(s32[32]{0:T(128)} %plen_hbm.1, s32[4,32]{1,0:T(4,128)} %bitcast.19, s32[32]{0:T(128)} %gp_hbm.1, bf16[8,128]{1,0:T(8,128)(2,1)} %hidden_hbm.1, f32[1,2048]{1,0:T(1,128)} %bitcast.17, f32[1,128]{1,0:T(1,128)} %bitcast.20, f32[1,128]{1,0:T(1,128)} %bitcast.21, ...), custom_call_target="tpu_custom_call" | custom-call | tf_op jit(solution)/shard_map/pallas_call | solution.py:421
  81.7 0.6 copy.24
  82.2 0.5 slice_bitcast_fusion

commit v5 on v4

--- a/solution.py
+++ b/solution.py
@@ -39,7 +39,7 @@
     wq_hbm, wg_hbm, wkv_hbm, wo_hbm, pk_hbm, pv_hbm, tk_hbm, tv_hbm, mg_hbm, mu_hbm, md_hbm,
     out_ref, score_ref,
     plen_ref, tlen_ref, gp_ref, again_ref, qgain_ref, kgain_ref, mgain_ref, fgain_ref, sw_ref,
-    wq, wg, wkv, wo, kc, vc, wmlp, wfar, wdown,
+    wq, wg, wkv, wo, kc, kt, vc, wmlp, wfar, wdown,
     hb, hf, qs, qb, qf, fs, fb, mb, mf, nb, nf, sb, rb, tb, xb, ps, pb, ds_, db, yb, zs, zb_, cs, cb, gs, gb,
     lsem, ssem, rsem, qsem,
 ):
@@ -123,9 +123,6 @@
 
     copies[0].wait()
     copies[1].wait()
-    send(wmlp.at[own_w], wfar, 13, 22, across)
-    for dy in (2, 1, 3):
-        send(wmlp.at[own_w], wmlp.at[own_w], 12, 21, (ys_[dy] * 8 + z, h))
     for dzq in (2, 3, 1):
         pl.semaphore_signal(qsem, inc=1, device_id=(y * 8 + zt * 4 + zqs[dzq], h), device_id_type=MESH)
     for i in range(2, 20):
@@ -169,6 +166,7 @@
         scaled = (value * again_ref[:, pl.ds(offset, 256)]).astype(BF)
         return value * value, scaled, offset
 
+    kt[...] = kc[...].T
     wait_recv(hb.at[pl.ds(0, 7)], 0)
     squares = jnp.zeros((8, 256), F32)
     q_acc = jnp.zeros((8, 128), F32)
@@ -197,11 +195,9 @@
     for dx, dc in NEAR:
         send(qs, qb.at[n], 1, 2, (r, head_at(dx, 0, dc)))
 
-    wait_recv(wfar, 22)
+    send(wmlp.at[own_w], wfar, 13, 22, across)
     for dy in (2, 1, 3):
-        send(wfar, wmlp.at[other_w], 8, 11, (ys_[dy] * 8 + z, h))
-    kept = pltpu.make_async_copy(wfar, wmlp.at[other_w], lsem.at[21])
-    kept.start()
+        send(wmlp.at[own_w], wmlp.at[own_w], 12, 21, (ys_[dy] * 8 + z, h))
 
     for scaled, offset in rest:
         g_acc = g_acc + dot(scaled, wg[pl.ds(offset, 256), :])
@@ -217,7 +213,7 @@
         q = queries[...].astype(F32).reshape(64, 128).astype(BF)
 
         def weights(keys, live):
-            scores = dot_nt(q, keys) * SCALE
+            scores = dot(q, keys) * SCALE
             rows = lax.broadcasted_iota(jnp.int32, scores.shape, 0)
             cols = lax.broadcasted_iota(jnp.int32, scores.shape, 1)
             seen = ((cols & 7) == (rows >> 4) * 2 + half) & live(rows, cols)
@@ -228,8 +224,8 @@
                               jnp.where(cols < 384, tails[2], tails[3])) - h * 16
             return ((cols >> 7) == ((rows & 7) >> 1)) & (((cols >> 3) & 15) < limit)
 
-        w_prefix = weights(kc[pl.ds(0, 2048), :], lambda rows, cols: (cols >> 3) < plen - h * 256)
-        w_tail = weights(kc[pl.ds(2048, 512), :], tail_live)
+        w_prefix = weights(kt[:, pl.ds(0, 2048)], lambda rows, cols: (cols >> 3) < plen - h * 256)
+        w_tail = weights(kt[:, pl.ds(2048, 512)], tail_live)
         numer = dot(w_prefix.astype(BF), vc[pl.ds(0, 2048), :]) + dot(w_tail.astype(BF), vc[pl.ds(2048, 512), :])
         total = jnp.sum(w_prefix, axis=-1, keepdims=True) + jnp.sum(w_tail, axis=-1, keepdims=True)
         high = total.astype(BF).astype(F32)
@@ -247,6 +243,12 @@
     attend(oh, qf, mf)
     for dx, dc in FAR:
         send(mf.at[near_at(dx, dc)], nf.at[n], 17, 6, (r, head_at(dx, 1, dc)))
+
+    wait_recv(wfar, 22)
+    for dy in (2, 1, 3):
+        send(wfar, wmlp.at[other_w], 8, 11, (ys_[dy] * 8 + z, h))
+    kept = pltpu.make_async_copy(wfar, wmlp.at[other_w], lsem.at[21])
+    kept.start()
 
     wait_recv(fb.at[0], 4)
     scores = dot_nt(query, fb[0]) * SCALE
@@ -428,7 +430,7 @@
             blocks(1, 2048, kind=F32), blocks(1, 128, kind=F32), blocks(1, 128, kind=F32),
             blocks(1, 2048, kind=F32), blocks(1, 128, kind=F32), blocks(1, 128, kind=F32),
             blocks(2048, 128), blocks(2048, 128), blocks(2048, 128), blocks(128, 2048),
-            blocks(2560, 128), blocks(2560, 128),
+            blocks(2560, 128), blocks(128, 2560), blocks(2560, 128),
             blocks(8, 64, 768), blocks(64, 768), blocks(384, 2048),
             blocks(8, 8, 128), blocks(8, 8, 128),
             blocks(8, 128), blocks(8, 8, 128), blocks(8, 8, 128),

time: 82.9 us -> 83 us (level)
  no operation moved by 1% of the time
where the time goes in v5:
time: 83 us; the launch traced here: 82.9 us
  Pallas kernels  81.2 us (98%)
  local copies, waits for them, and re-layouts  1.09 us (1%)
    pallas_call x1, Pallas kernels, shards(): pl.pallas_call(kernel, out_shape=(pltpu.VMEM((8, 128), BF), pltpu.VMEM((1...  81.2 us

profile of v5, /device:TPU:1, one launch (start us, length us, event | category | flops | bytes accessed | tf_op | source)
XLA Modules:
  0.0 82.9 jit_solution(2694756449477921630)
XLA Ops:
  0.6 81.2 %shard_map.212 = (bf16[8,128]{1,0:T(8,128)(2,1)S(1)}, f32[1,128]{1,0:T(1,128)S(1)}) custom-call(s32[32]{0:T(128)} %plen_hbm.1, s32[4,32]{1,0:T(4,128)} %bitcast.19, s32[32]{0:T(128)} %gp_hbm.1, bf16[8,128]{1,0:T(8,128)(2,1)} %hidden_hbm.1, f32[1,2048]{1,0:T(1,128)} %bitcast.17, f32[1,128]{1,0:T(1,128)} %bitcast.20, f32[1,128]{1,0:T(1,128)} %bitcast.21, ...), custom_call_target="tpu_custom_call" | custom-call | tf_op jit(solution)/shard_map/pallas_call | solution.py:423
  81.8 0.6 copy.24
  82.4 0.5 slice_bitcast_fusion
